TPU v7x, 32 devices: a whole 2x2x4 slice. The times are simulated.
32 devices in a mesh: member: 4 (over y, x), lat: 8 (over z, core).
Axes of the slice: x: 2, y: 2, z: 4, core: 2. Of those that a mesh axis runs over, the one named last changes fastest.
Arguments:
- fields: bfloat16 [4, 641, 16, 720], P('member', None, 'lat'), as said below
- noise_fields: bfloat16 [4, 8, 16, 720], P('member', None, 'lat'), may hold values from -5 to 5
- target_fields: bfloat16 [641, 16, 720], P(None, 'lat'), as said below
- band_heights: int32 [8], replicated, may hold values from 1 to 2
- tap_offsets: int32 [9, 16], P(None, 'lat'), may hold values from -8 to 8
- expand_weight: float32 [641, 1282], replicated, may hold values from -0.25 to 0.25
- expand_bias: float32 [1282], replicated, may hold values from -1.75 to 1.75
- reduce_weight: float32 [1282, 641], replicated, may hold values from -0.15625 to 0.15625
- channel_vectors: float32 [2, 641], replicated, as said below
- disco_filter: float32 [9, 641], replicated, may hold values from -2 to 2
- noise_mixing: float32 [8, 641], replicated, may hold values from -2 to 2
- first_expand: float32 [641, 1282], replicated, may hold values from -0.5 to 0.5
- second_expand: float32 [641, 1282], replicated, may hold values from 0.029994337 to 0.11997735
- first_bias: float32 [1282], replicated, may hold values from -0.5 to 0.5
- second_bias: float32 [1282], replicated, may hold values from 0.029994337 to 0.11997735
- first_reduce: float32 [1282, 641], replicated, may hold values from -0.5 to 0.5
- second_reduce: float32 [1282, 641], replicated, may hold values from 0.029994337 to 0.11997735
- first_vectors: float32 [2, 641], replicated, may hold values from -0.5 to 0.5
- second_vectors: float32 [2, 641], replicated, may hold values from 0.029994337 to 0.11997735
- first_filter: float32 [9, 641], replicated, may hold values from -0.5 to 0.5
- second_filter: float32 [9, 641], replicated, may hold values from 0.029994337 to 0.11997735
- first_mixing: float32 [8, 641], replicated, may hold values from -0.5 to 0.5
- second_mixing: float32 [8, 641], replicated, may hold values from 0.029994337 to 0.11997735
Outputs:
- mean_loss: float32 [], replicated
- input_gradient: bfloat16 [4, 641, 16, 720], P('member', None, 'lat')
- gradient_norm: float32 [], replicated
- expand_out: float32 [641, 1282], replicated
- expand_first: float32 [641, 1282], replicated
- expand_second: float32 [641, 1282], replicated
- bias_out: float32 [1282], replicated
- bias_first: float32 [1282], replicated
- bias_second: float32 [1282], replicated
- reduce_out: float32 [1282, 641], replicated
- reduce_first: float32 [1282, 641], replicated
- reduce_second: float32 [1282, 641], replicated
- vectors_out: float32 [2, 641], replicated
- vectors_first: float32 [2, 641], replicated
- vectors_second: float32 [2, 641], replicated
- filter_out: float32 [9, 641], replicated
- filter_first: float32 [9, 641], replicated
- filter_second: float32 [9, 641], replicated
- mixing_out: float32 [8, 641], replicated
- mixing_first: float32 [8, 641], replicated
- mixing_second: float32 [8, 641], replicated
- expand_copy: bfloat16 [641, 1282], replicated
- reduce_copy: bfloat16 [1282, 641], replicated
Inputs may be any that keep to these rules, and one draw needn't show every extreme that they name: `band_heights`: each band has 1 or 2 live rows. `fields`: finite values. `target_fields`: finite values. `channel_vectors`: gains positive, biases of either sign.
All inputs are finite; a program needn't handle non-finite values.
Results may differ from a plain program's by a relative error of at most 0.0085.
Values may be sent and summed in bfloat16 or wider, within the bound.
No kernel may reach another device: no remote copies, remote signals or barrier semaphores. Data moves between devices by JAX's collectives and lax.ppermute only.
A program may use at most 384 MiB of HBM per device.

v0:
```python
import math

import jax
import jax.numpy as jnp
from jax import lax
from jax.sharding import PartitionSpec as P

MAXOFF = 8
STEP = 10


BETA_ONE = 0.9
BETA_TWO = 0.95
ADAM_EPS = 1e-08
DECAY_RATE = 0.1
NORM_EPS = 1e-05
SMALL_RATE = 0.3
HIGHEST = lax.Precision.HIGHEST


def padded(shard, sides, width):
    for axis, dim in sides:
        count, length = (lax.axis_size(axis), shard.shape[dim])
        up = [(i, (i + 1) % count) for i in range(count - 1)]
        down = [(j, i) for i, j in up]
        last = lax.slice_in_dim(shard, length - width, length, axis=dim)
        leading = lax.slice_in_dim(shard, 0, width, axis=dim)
        before = lax.ppermute(last, axis, up)
        after = lax.ppermute(leading, axis, down)
        shard = jnp.concatenate([before, shard, after], axis=dim)
    return shard


def smooth_abs(values):
    return jnp.sqrt(values * values + 1.0)


def smooth_slope(values):
    return values / jnp.sqrt(values * values + 1.0)


def gelu_exact(values):
    return jax.nn.gelu(values, approximate=False)


def layer_norm(values, norm_gain):
    gain_shape = (1, -1) + (1,) * (values.ndim - 2)
    centre = jnp.mean(values, axis=1, keepdims=True)
    centred = values - centre
    spread = jnp.mean(centred * centred, axis=1, keepdims=True)
    return centred * lax.rsqrt(spread + NORM_EPS) * norm_gain.reshape(gain_shape)


def wrap_lon(anchor):
    margin = MAXOFF
    lon_count = anchor.shape[4]
    return jnp.concatenate(
        [anchor[:, :, :, :, lon_count - margin :], anchor, anchor[:, :, :, :, :margin]], axis=4
    )


def shift_rows(extended, tap_row, lon_count):

    def one_row(row_data, start):
        return lax.dynamic_slice_in_dim(row_data, start, lon_count, axis=3)

    starts = tap_row + MAXOFF
    return jax.vmap(one_row, in_axes=(3, 0), out_axes=3)(extended, starts)


def disco(source, prev_row, next_row, height, offsets, weights):
    row_count = source.shape[3]
    lon_count = source.shape[4]
    row_ids = jnp.arange(row_count, dtype=jnp.int32)
    live_rows = (row_ids < height).astype(jnp.float32)[None, None, None, :, None]
    last_row = (row_ids == height - 1)[None, None, None, :, None]
    upper_rows = (
        jnp.concatenate([prev_row[:, :, :, None, :], source[:, :, :, :-1, :]], axis=3) * live_rows
    )
    shifted = jnp.concatenate(
        [source[:, :, :, 1:, :], jnp.zeros_like(source[:, :, :, :1, :])], axis=3
    )
    lower_rows = jnp.where(last_row, next_row[:, :, :, None, :], shifted) * live_rows
    result = jnp.zeros_like(source)
    for lat_tap, anchor in enumerate((upper_rows, source, lower_rows)):
        extended = wrap_lon(anchor)
        for lon_tap in range(3):
            tap_index = 3 * lat_tap + lon_tap
            moved = shift_rows(extended, offsets[tap_index], lon_count)
            result = result + weights[tap_index][None, :, None, None, None] * moved
    return result


def adam_step(weight, gradient, first, second, rate):
    first_new = BETA_ONE * first + (1.0 - BETA_ONE) * gradient
    second_new = BETA_TWO * second + (1.0 - BETA_TWO) * gradient * gradient
    first_hat = first_new / (1.0 - BETA_ONE**STEP)
    second_hat = second_new / (1.0 - BETA_TWO**STEP)
    weight_new = weight - rate * (
        first_hat / (jnp.sqrt(second_hat) + ADAM_EPS) + DECAY_RATE * weight
    )
    return (weight_new, first_new, second_new)


def on_device(
    fields,
    noise_fields,
    target_fields,
    band_heights,
    tap_offsets,
    expand_weight,
    expand_bias,
    reduce_weight,
    channel_vectors,
    disco_filter,
    noise_mixing,
    first_expand,
    second_expand,
    first_bias,
    second_bias,
    first_reduce,
    second_reduce,
    first_vectors,
    second_vectors,
    first_filter,
    second_filter,
    first_mixing,
    second_mixing,
):
    members_here = fields.shape[0]
    ensemble = members_here * lax.axis_size("member")
    lat_count = lax.axis_size("lat")
    row_count = fields.shape[2]
    lon_count = fields.shape[3]
    channels = expand_weight.shape[0]
    hidden = expand_weight.shape[1]
    band_index = lax.axis_index("lat")
    height = lax.dynamic_slice_in_dim(band_heights, band_index, 1)
    row_ids = jnp.arange(row_count, dtype=jnp.int32)
    column = (1, -1, 1, 1, 1)
    inputs = fields.astype(jnp.float32)[:, :, None]
    normed32, norm_back = jax.vjp(layer_norm, inputs, channel_vectors[0])
    normed = normed32.astype(jnp.bfloat16)
    bottom = lax.dynamic_slice_in_dim(normed, height[0] - 1, 1, axis=3)
    edges = jnp.concatenate([normed[:, :, :, 0:1], bottom], axis=3)[:, :, 0]
    bordered = padded(edges, (("lat", 2),), 1)
    prev_row = bordered[:, :, 0:1].astype(jnp.float32)
    next_row = bordered[:, :, 3:4].astype(jnp.float32)

    def conv_local(source, before_rows, after_rows, weights):
        return disco(source, before_rows, after_rows, height[0], tap_offsets, weights)

    filtered, conv_back = jax.vjp(
        conv_local, normed.astype(jnp.float32), prev_row, next_row, disco_filter
    )
    noise32 = noise_fields.astype(jnp.float32)[:, :, None]
    mixed_low = (
        filtered + jnp.einsum("kc,ekgrl->ecgrl", noise_mixing, noise32, precision=HIGHEST)
    ).astype(jnp.bfloat16)
    expand_low = expand_weight.astype(jnp.bfloat16)
    reduce_low = reduce_weight.astype(jnp.bfloat16)
    pre_act = jnp.einsum(
        "ch,ecgrl->ehgrl", expand_low, mixed_low, preferred_element_type=jnp.float32
    ) + expand_bias.reshape(column)
    activation32, gelu_back = jax.vjp(gelu_exact, pre_act)
    activation = activation32.astype(jnp.bfloat16)
    branch = jnp.einsum(
        "hc,ehgrl->ecgrl", reduce_low, activation, preferred_element_type=jnp.float32
    ) + channel_vectors[1].reshape(column)
    predicted = inputs + branch
    live_rows = (row_ids < height[0]).astype(jnp.float32)[None, None, None, :, None]
    target_gap = predicted - target_fields.astype(jnp.float32)[None, :, None]
    everyone = lax.all_gather(predicted, "member", axis=0, tiled=True)
    differences = predicted[:, None] - everyone[None]
    pair_sum = jnp.sum(smooth_abs(differences), axis=1)
    pair_slope = jnp.sum(smooth_slope(differences), axis=1)
    pair_loss = jnp.sum(live_rows * pair_sum)
    loss_local = jnp.sum(live_rows * smooth_abs(target_gap)) / ensemble - pair_loss / (
        2.0 * ensemble * ensemble
    )
    grad_pred = live_rows * (
        smooth_slope(target_gap) / ensemble - pair_slope / (ensemble * ensemble)
    )
    branch_grad = grad_pred.astype(jnp.bfloat16)
    grad_out_bias = jnp.sum(branch_grad, axis=(0, 2, 3, 4), dtype=jnp.float32)
    grad_reduce = jnp.einsum(
        "ehgrl,ecgrl->hc", activation, branch_grad, preferred_element_type=jnp.float32
    )
    grad_act = jnp.einsum(
        "hc,ecgrl->ehgrl", reduce_low, branch_grad, preferred_element_type=jnp.float32
    )
    (grad_pre,) = gelu_back(grad_act)
    pre_grad = grad_pre.astype(jnp.bfloat16)
    grad_bias_in = jnp.sum(pre_grad, axis=(0, 2, 3, 4), dtype=jnp.float32)
    grad_expand = jnp.einsum(
        "ecgrl,ehgrl->ch", mixed_low, pre_grad, preferred_element_type=jnp.float32
    )
    grad_mixed = jnp.einsum(
        "ch,ehgrl->ecgrl", expand_low, pre_grad, preferred_element_type=jnp.float32
    )
    grad_mixing = jnp.einsum("ecgrl,ekgrl->kc", grad_mixed, noise32, precision=HIGHEST)
    grad_normed, grad_before, grad_after, grad_filter = conv_back(grad_mixed)
    returned = padded(
        jnp.concatenate([grad_before, grad_after], axis=2).astype(jnp.bfloat16), (("lat", 2),), 1
    ).astype(jnp.float32)
    first_row = (row_ids == 0)[None, None, None, :, None]
    final_row = (row_ids == height[0] - 1)[None, None, None, :, None]
    grad_normed = grad_normed + jnp.where(first_row, returned[:, :, 0:1][:, :, :, None, :], 0.0)
    grad_normed = grad_normed + jnp.where(final_row, returned[:, :, 3:4][:, :, :, None, :], 0.0)
    grad_inputs, grad_gain = norm_back(grad_normed)
    input_gradient = (grad_pred + grad_inputs)[:, :, 0].astype(jnp.bfloat16)
    (
        sum_expand,
        sum_bias_in,
        sum_reduce,
        sum_gain,
        sum_bias_out,
        sum_filter,
        sum_mixing,
        loss_total,
    ) = lax.psum(
        (
            grad_expand,
            grad_bias_in,
            grad_reduce,
            grad_gain,
            grad_out_bias,
            grad_filter,
            grad_mixing,
            loss_local,
        ),
        ("member", "lat"),
    )
    sum_vectors = jnp.stack([sum_gain, sum_bias_out])
    live_total = jnp.sum(band_heights).astype(jnp.float32)
    mean_loss = loss_total / (channels * lon_count * live_total)
    squares = (
        jnp.sum(sum_expand * sum_expand)
        + jnp.sum(sum_bias_in * sum_bias_in)
        + jnp.sum(sum_reduce * sum_reduce)
    )
    squares = (
        squares
        + jnp.sum(sum_vectors * sum_vectors)
        + jnp.sum(sum_filter * sum_filter)
        + jnp.sum(sum_mixing * sum_mixing)
    )
    gradient_norm = jnp.sqrt(squares)
    limit = 0.02 * math.sqrt(hidden * channels * lat_count * row_count * lon_count / ensemble)
    factor = jnp.minimum(1.0, limit / (gradient_norm + 1e-06))
    expand_out, expand_first, expand_second = adam_step(
        expand_weight, factor * sum_expand, first_expand, second_expand, channels ** (-0.5)
    )
    bias_out, bias_first, bias_second = adam_step(
        expand_bias, factor * sum_bias_in, first_bias, second_bias, SMALL_RATE
    )
    reduce_out, reduce_first, reduce_second = adam_step(
        reduce_weight, factor * sum_reduce, first_reduce, second_reduce, hidden ** (-0.5)
    )
    vectors_out, vectors_first, vectors_second = adam_step(
        channel_vectors, factor * sum_vectors, first_vectors, second_vectors, SMALL_RATE
    )
    filter_out, filter_first, filter_second = adam_step(
        disco_filter, factor * sum_filter, first_filter, second_filter, SMALL_RATE
    )
    mixing_out, mixing_first, mixing_second = adam_step(
        noise_mixing, factor * sum_mixing, first_mixing, second_mixing, SMALL_RATE
    )
    return (
        mean_loss,
        input_gradient,
        gradient_norm,
        expand_out,
        expand_first,
        expand_second,
        bias_out,
        bias_first,
        bias_second,
        reduce_out,
        reduce_first,
        reduce_second,
        vectors_out,
        vectors_first,
        vectors_second,
        filter_out,
        filter_first,
        filter_second,
        mixing_out,
        mixing_first,
        mixing_second,
        expand_out.astype(jnp.bfloat16),
        reduce_out.astype(jnp.bfloat16),
    )


def solution(mesh):
    in_specs = (
        P("member", None, "lat", None),
        P("member", None, "lat", None),
        P(None, "lat", None),
        P(),
        P(None, "lat"),
        P(),
        P(),
        P(),
        P(),
        P(),
        P(),
        P(),
        P(),
        P(),
        P(),
        P(),
        P(),
        P(),
        P(),
        P(),
        P(),
        P(),
        P(),
    )
    out_specs = (
        P(),
        P("member", None, "lat", None),
        P(),
        P(),
        P(),
        P(),
        P(),
        P(),
        P(),
        P(),
        P(),
        P(),
        P(),
        P(),
        P(),
        P(),
        P(),
        P(),
        P(),
        P(),
        P(),
        P(),
        P(),
    )
    return jax.shard_map(
        on_device, mesh=mesh, in_specs=in_specs, out_specs=out_specs, check_vma=False
    )
```

profile of v0, /device:TPU:0, one launch (start us, length us, event | category | flops | bytes accessed | tf_op | source)
XLA Modules:
  0.0 3593.1 jit_solution(16687512212526045180)
XLA Ops:
  41.3 17.9 while.21
  42.1 8.4 dynamic-slice_dynamic-update-slice_fusion.21
  63.3 18.0 while.22
  63.9 8.3 dynamic-slice_dynamic-update-slice_fusion.22
  72.8 8.3 dynamic-slice_dynamic-update-slice_fusion.22
  85.2 17.7 while.23
  85.7 8.2 dynamic-slice_dynamic-update-slice_fusion.23
  94.6 8.3 dynamic-slice_dynamic-update-slice_fusion.23
  124.6 17.8 while.24
  125.2 8.3 dynamic-slice_dynamic-update-slice_fusion.24
  134.1 8.2 dynamic-slice_dynamic-update-slice_fusion.24
  146.4 17.9 while.25
  155.8 8.3 dynamic-slice_dynamic-update-slice_fusion.25
  176.4 18.0 while.18
  185.8 8.3 dynamic-slice_dynamic-update-slice_fusion.18
  198.4 17.6 while.19
  207.8 8.2 dynamic-slice_dynamic-update-slice_fusion.19
  220.0 17.8 while.20
  229.6 8.3 dynamic-slice_dynamic-update-slice_fusion.20
  241.8 17.7 while.26
  242.4 8.2 dynamic-slice_dynamic-update-slice_fusion.26
  251.2 8.3 dynamic-slice_dynamic-update-slice_fusion.26
  259.5 24.9 fusion.47
  290.5 22.3 fusion.23
  327.7 143.7 %all-gather.2.cloned.1.call-done = f32[4,641,1,2,720]{4,3,2,1,0:T(2,128)} async-done(((f32[1,641,1,2,720]{4,3,2,1,0:T(2,128)}), f32[4,641,1,2,720]{4,3,2,1,0:T(2,128)}) %all-gather.2.cloned.1.call-update) | async-done | bytes 14768656 | tf_op jit(solution)/shard_map/all_gather | solution.py:173
  471.4 47.2 %multiply_reduce_fusion = (f32[641,2,720]{2,1,0:T(2,128)S(1)}, f32[641,2,720]{2,1,0:T(2,128)}) fusion(f32[4,641,1,2,720]{4,3,2,1,0:T(2,128)} %all-gather.2.cloned.1.call-done, f32[641,2,720]{2,1,0:T(2,128)} %copy.230), kind=kLoop, calls=%fused_computation.45 | loop fusion | flops 20306880 | bytes 25845120 | tf_op jit(solution)/shard_map/reduce_sum | solution.py:176
  523.6 28.0 convert_reduce_fusion
  551.6 22.5 fusion.48
  574.0 13.3 fusion.59
  597.3 291.2 %while.33 = (s32[]{:T(128)}, f32[2,1,641,1,736]{4,3,2,1,0:T(1,128)}, s32[2,5]{1,0:T(2,128)S(1)}, f32[2,1,641,1,720]{4,3,2,1,0:T(1,128)}, s32[]{:T(128)}, /*index=5*/s32[5]{0:T(128)S(1)}, s32[]{:T(128)}) while((s32[]{:T(128)}, f32[2,1,641,1,736]{4,3,2,1,0:T(1,128)}, s32[2,5]{1,0:T(2,128)S(1)}, f32[2,1,641,1,720]{4,3,2,1,0:T(1,128)}, s32[]{:T(128)}, ...), condition=%wide.while_cond.15, body=%wide.while_body.15.sunk | while | flops 923061 | bytes 9230659 | solution.py:65
  610.1 132.6 %dynamic-update-slice.78 = f32[2,1,641,1,736]{4,3,2,1,0:T(1,128)} dynamic-update-slice(f32[2,1,641,1,736]{4,3,2,1,0:T(1,128)} %get-tuple-element.1594, f32[1,1,641,1,720]{4,3,2,1,0:T(1,128)S(1)} %broadcast_select_fusion.24, s32[]{:T(128)} %bitcast.665, s32[]{:T(128)} %constant.58.clone.1..sunk.6, s32[]{:T(128)} %constant.58.clone.1..sunk.6, s32[]{:T(128)} %constant.58.clone.1..sunk.6, s32[]{:T(128)} %bitcast.666) | dynamic-update-slice | bytes 3692164 | tf_op jit(solution)/shard_map/transpose(jvp(vmap()))/scatter-add
  755.5 132.7 %dynamic-update-slice.78 = f32[2,1,641,1,736]{4,3,2,1,0:T(1,128)} dynamic-update-slice(f32[2,1,641,1,736]{4,3,2,1,0:T(1,128)} %get-tuple-element.1594, f32[1,1,641,1,720]{4,3,2,1,0:T(1,128)S(1)} %broadcast_select_fusion.24, s32[]{:T(128)} %bitcast.665, s32[]{:T(128)} %constant.58.clone.1..sunk.6, s32[]{:T(128)} %constant.58.clone.1..sunk.6, s32[]{:T(128)} %constant.58.clone.1..sunk.6, s32[]{:T(128)} %bitcast.666) | dynamic-update-slice | bytes 3692164 | tf_op jit(solution)/shard_map/transpose(jvp(vmap()))/scatter-add
  900.5 291.1 %while.34 = (s32[]{:T(128)}, f32[2,1,641,1,736]{4,3,2,1,0:T(1,128)}, s32[2,5]{1,0:T(2,128)S(1)}, f32[2,1,641,1,720]{4,3,2,1,0:T(1,128)}, s32[]{:T(128)}, /*index=5*/s32[5]{0:T(128)S(1)}, s32[]{:T(128)}) while((s32[]{:T(128)}, f32[2,1,641,1,736]{4,3,2,1,0:T(1,128)}, s32[2,5]{1,0:T(2,128)S(1)}, f32[2,1,641,1,720]{4,3,2,1,0:T(1,128)}, s32[]{:T(128)}, ...), condition=%wide.while_cond.16, body=%wide.while_body.16.sunk | while | flops 923061 | bytes 9230659 | solution.py:65
  913.4 132.6 %dynamic-update-slice.79 = f32[2,1,641,1,736]{4,3,2,1,0:T(1,128)} dynamic-update-slice(f32[2,1,641,1,736]{4,3,2,1,0:T(1,128)} %get-tuple-element.1615, f32[1,1,641,1,720]{4,3,2,1,0:T(1,128)S(1)} %broadcast_select_fusion.25, s32[]{:T(128)} %bitcast.672, s32[]{:T(128)} %constant.58.clone.1..sunk.7, s32[]{:T(128)} %constant.58.clone.1..sunk.7, s32[]{:T(128)} %constant.58.clone.1..sunk.7, s32[]{:T(128)} %bitcast.673) | dynamic-update-slice | bytes 3692164 | tf_op jit(solution)/shard_map/transpose(jvp(vmap()))/scatter-add
  1058.9 132.6 %dynamic-update-slice.79 = f32[2,1,641,1,736]{4,3,2,1,0:T(1,128)} dynamic-update-slice(f32[2,1,641,1,736]{4,3,2,1,0:T(1,128)} %get-tuple-element.1615, f32[1,1,641,1,720]{4,3,2,1,0:T(1,128)S(1)} %broadcast_select_fusion.25, s32[]{:T(128)} %bitcast.672, s32[]{:T(128)} %constant.58.clone.1..sunk.7, s32[]{:T(128)} %constant.58.clone.1..sunk.7, s32[]{:T(128)} %constant.58.clone.1..sunk.7, s32[]{:T(128)} %bitcast.673) | dynamic-update-slice | bytes 3692164 | tf_op jit(solution)/shard_map/transpose(jvp(vmap()))/scatter-add
  1199.7 9.2 add_any.94
  1209.0 291.0 %while.35 = (s32[]{:T(128)}, f32[2,1,641,1,736]{4,3,2,1,0:T(1,128)}, s32[2,5]{1,0:T(2,128)S(1)}, f32[2,1,641,1,720]{4,3,2,1,0:T(1,128)}, s32[]{:T(128)}, /*index=5*/s32[5]{0:T(128)S(1)}, s32[]{:T(128)}) while((s32[]{:T(128)}, f32[2,1,641,1,736]{4,3,2,1,0:T(1,128)}, s32[2,5]{1,0:T(2,128)S(1)}, f32[2,1,641,1,720]{4,3,2,1,0:T(1,128)}, s32[]{:T(128)}, ...), condition=%wide.while_cond.17, body=%wide.while_body.17.sunk | while | flops 923061 | bytes 9230659 | solution.py:65
  1222.0 132.6 %dynamic-update-slice.80 = f32[2,1,641,1,736]{4,3,2,1,0:T(1,128)} dynamic-update-slice(f32[2,1,641,1,736]{4,3,2,1,0:T(1,128)} %get-tuple-element.1636, f32[1,1,641,1,720]{4,3,2,1,0:T(1,128)S(1)} %broadcast_select_fusion.26, s32[]{:T(128)} %bitcast.679, s32[]{:T(128)} %constant.58.clone.1..sunk.8, s32[]{:T(128)} %constant.58.clone.1..sunk.8, s32[]{:T(128)} %constant.58.clone.1..sunk.8, s32[]{:T(128)} %bitcast.680) | dynamic-update-slice | bytes 3692164 | tf_op jit(solution)/shard_map/transpose(jvp(vmap()))/scatter-add
  1367.4 132.6 %dynamic-update-slice.80 = f32[2,1,641,1,736]{4,3,2,1,0:T(1,128)} dynamic-update-slice(f32[2,1,641,1,736]{4,3,2,1,0:T(1,128)} %get-tuple-element.1636, f32[1,1,641,1,720]{4,3,2,1,0:T(1,128)S(1)} %broadcast_select_fusion.26, s32[]{:T(128)} %bitcast.679, s32[]{:T(128)} %constant.58.clone.1..sunk.8, s32[]{:T(128)} %constant.58.clone.1..sunk.8, s32[]{:T(128)} %constant.58.clone.1..sunk.8, s32[]{:T(128)} %bitcast.680) | dynamic-update-slice | bytes 3692164 | tf_op jit(solution)/shard_map/transpose(jvp(vmap()))/scatter-add
  1515.7 290.7 %while.31 = (s32[]{:T(128)}, f32[2,1,641,1,736]{4,3,2,1,0:T(1,128)}, s32[2,5]{1,0:T(2,128)S(1)}, f32[2,1,641,1,720]{4,3,2,1,0:T(1,128)}, s32[]{:T(128)}, /*index=5*/s32[5]{0:T(128)S(1)}, s32[]{:T(128)}) while((s32[]{:T(128)}, f32[2,1,641,1,736]{4,3,2,1,0:T(1,128)}, s32[2,5]{1,0:T(2,128)S(1)}, f32[2,1,641,1,720]{4,3,2,1,0:T(1,128)}, s32[]{:T(128)}, ...), condition=%wide.while_cond.13, body=%wide.while_body.13.sunk | while | flops 923061 | bytes 9230659 | solution.py:65
  1528.7 132.6 %dynamic-update-slice.76 = f32[2,1,641,1,736]{4,3,2,1,0:T(1,128)} dynamic-update-slice(f32[2,1,641,1,736]{4,3,2,1,0:T(1,128)} %get-tuple-element.1552, f32[1,1,641,1,720]{4,3,2,1,0:T(1,128)S(1)} %broadcast_select_fusion.22, s32[]{:T(128)} %bitcast.651, s32[]{:T(128)} %constant.58.clone.1..sunk.4, s32[]{:T(128)} %constant.58.clone.1..sunk.4, s32[]{:T(128)} %constant.58.clone.1..sunk.4, s32[]{:T(128)} %bitcast.652) | dynamic-update-slice | bytes 3692164 | tf_op jit(solution)/shard_map/transpose(jvp(vmap()))/scatter-add
  1673.8 132.6 %dynamic-update-slice.76 = f32[2,1,641,1,736]{4,3,2,1,0:T(1,128)} dynamic-update-slice(f32[2,1,641,1,736]{4,3,2,1,0:T(1,128)} %get-tuple-element.1552, f32[1,1,641,1,720]{4,3,2,1,0:T(1,128)S(1)} %broadcast_select_fusion.22, s32[]{:T(128)} %bitcast.651, s32[]{:T(128)} %constant.58.clone.1..sunk.4, s32[]{:T(128)} %constant.58.clone.1..sunk.4, s32[]{:T(128)} %constant.58.clone.1..sunk.4, s32[]{:T(128)} %bitcast.652) | dynamic-update-slice | bytes 3692164 | tf_op jit(solution)/shard_map/transpose(jvp(vmap()))/scatter-add
  1818.4 290.5 %while.30 = (s32[]{:T(128)}, f32[2,1,641,1,736]{4,3,2,1,0:T(1,128)}, s32[2,5]{1,0:T(2,128)S(1)}, f32[2,1,641,1,720]{4,3,2,1,0:T(1,128)}, s32[]{:T(128)}, /*index=5*/s32[5]{0:T(128)S(1)}, s32[]{:T(128)}) while((s32[]{:T(128)}, f32[2,1,641,1,736]{4,3,2,1,0:T(1,128)}, s32[2,5]{1,0:T(2,128)S(1)}, f32[2,1,641,1,720]{4,3,2,1,0:T(1,128)}, s32[]{:T(128)}, ...), condition=%wide.while_cond.12, body=%wide.while_body.12.sunk | while | flops 923061 | bytes 9230659 | solution.py:65
  1831.3 132.5 %dynamic-update-slice.75 = f32[2,1,641,1,736]{4,3,2,1,0:T(1,128)} dynamic-update-slice(f32[2,1,641,1,736]{4,3,2,1,0:T(1,128)} %get-tuple-element.1531, f32[1,1,641,1,720]{4,3,2,1,0:T(1,128)S(1)} %broadcast_select_fusion.21, s32[]{:T(128)} %bitcast.644, s32[]{:T(128)} %constant.58.clone.1..sunk.3, s32[]{:T(128)} %constant.58.clone.1..sunk.3, s32[]{:T(128)} %constant.58.clone.1..sunk.3, s32[]{:T(128)} %bitcast.645) | dynamic-update-slice | bytes 3692164 | tf_op jit(solution)/shard_map/transpose(jvp(vmap()))/scatter-add
  1976.4 132.5 %dynamic-update-slice.75 = f32[2,1,641,1,736]{4,3,2,1,0:T(1,128)} dynamic-update-slice(f32[2,1,641,1,736]{4,3,2,1,0:T(1,128)} %get-tuple-element.1531, f32[1,1,641,1,720]{4,3,2,1,0:T(1,128)S(1)} %broadcast_select_fusion.21, s32[]{:T(128)} %bitcast.644, s32[]{:T(128)} %constant.58.clone.1..sunk.3, s32[]{:T(128)} %constant.58.clone.1..sunk.3, s32[]{:T(128)} %constant.58.clone.1..sunk.3, s32[]{:T(128)} %bitcast.645) | dynamic-update-slice | bytes 3692164 | tf_op jit(solution)/shard_map/transpose(jvp(vmap()))/scatter-add
  2117.0 9.2 add_any.89
  2126.3 290.8 %while.32 = (s32[]{:T(128)}, f32[2,1,641,1,736]{4,3,2,1,0:T(1,128)}, s32[2,5]{1,0:T(2,128)S(1)}, f32[2,1,641,1,720]{4,3,2,1,0:T(1,128)}, s32[]{:T(128)}, /*index=5*/s32[5]{0:T(128)S(1)}, s32[]{:T(128)}) while((s32[]{:T(128)}, f32[2,1,641,1,736]{4,3,2,1,0:T(1,128)}, s32[2,5]{1,0:T(2,128)S(1)}, f32[2,1,641,1,720]{4,3,2,1,0:T(1,128)}, s32[]{:T(128)}, ...), condition=%wide.while_cond.14, body=%wide.while_body.14.sunk | while | flops 923061 | bytes 9230659 | solution.py:65
  2139.2 132.6 %dynamic-update-slice.77 = f32[2,1,641,1,736]{4,3,2,1,0:T(1,128)} dynamic-update-slice(f32[2,1,641,1,736]{4,3,2,1,0:T(1,128)} %get-tuple-element.1573, f32[1,1,641,1,720]{4,3,2,1,0:T(1,128)S(1)} %broadcast_select_fusion.23, s32[]{:T(128)} %bitcast.658, s32[]{:T(128)} %constant.58.clone.1..sunk.5, s32[]{:T(128)} %constant.58.clone.1..sunk.5, s32[]{:T(128)} %constant.58.clone.1..sunk.5, s32[]{:T(128)} %bitcast.659) | dynamic-update-slice | bytes 3692164 | tf_op jit(solution)/shard_map/transpose(jvp(vmap()))/scatter-add
  2284.5 132.6 %dynamic-update-slice.77 = f32[2,1,641,1,736]{4,3,2,1,0:T(1,128)} dynamic-update-slice(f32[2,1,641,1,736]{4,3,2,1,0:T(1,128)} %get-tuple-element.1573, f32[1,1,641,1,720]{4,3,2,1,0:T(1,128)S(1)} %broadcast_select_fusion.23, s32[]{:T(128)} %bitcast.658, s32[]{:T(128)} %constant.58.clone.1..sunk.5, s32[]{:T(128)} %constant.58.clone.1..sunk.5, s32[]{:T(128)} %constant.58.clone.1..sunk.5, s32[]{:T(128)} %bitcast.659) | dynamic-update-slice | bytes 3692164 | tf_op jit(solution)/shard_map/transpose(jvp(vmap()))/scatter-add
  2429.7 20.7 convolution_bitcast_fusion
  2455.9 8.3 copy.236
  2468.1 291.1 %while.27 = (s32[]{:T(128)}, f32[2,1,641,1,736]{4,3,2,1,0:T(1,128)}, s32[2,5]{1,0:T(2,128)S(1)}, f32[2,1,641,1,720]{4,3,2,1,0:T(1,128)}, s32[]{:T(128)}, /*index=5*/s32[5]{0:T(128)S(1)}, s32[]{:T(128)}) while((s32[]{:T(128)}, f32[2,1,641,1,736]{4,3,2,1,0:T(1,128)}, s32[2,5]{1,0:T(2,128)S(1)}, f32[2,1,641,1,720]{4,3,2,1,0:T(1,128)}, s32[]{:T(128)}, ...), condition=%wide.while_cond.9, body=%wide.while_body.9.sunk | while | flops 923061 | bytes 9230659 | solution.py:65
  2480.9 132.6 %dynamic-update-slice.72 = f32[2,1,641,1,736]{4,3,2,1,0:T(1,128)} dynamic-update-slice(f32[2,1,641,1,736]{4,3,2,1,0:T(1,128)} %get-tuple-element.1657, f32[1,1,641,1,720]{4,3,2,1,0:T(1,128)S(1)} %broadcast_select_fusion.18, s32[]{:T(128)} %bitcast.623, s32[]{:T(128)} %constant.58.clone.1..sunk, s32[]{:T(128)} %constant.58.clone.1..sunk, s32[]{:T(128)} %constant.58.clone.1..sunk, s32[]{:T(128)} %bitcast.624) | dynamic-update-slice | bytes 3692164 | tf_op jit(solution)/shard_map/transpose(jvp(vmap()))/scatter-add
  2626.2 132.6 %dynamic-update-slice.72 = f32[2,1,641,1,736]{4,3,2,1,0:T(1,128)} dynamic-update-slice(f32[2,1,641,1,736]{4,3,2,1,0:T(1,128)} %get-tuple-element.1657, f32[1,1,641,1,720]{4,3,2,1,0:T(1,128)S(1)} %broadcast_select_fusion.18, s32[]{:T(128)} %bitcast.623, s32[]{:T(128)} %constant.58.clone.1..sunk, s32[]{:T(128)} %constant.58.clone.1..sunk, s32[]{:T(128)} %constant.58.clone.1..sunk, s32[]{:T(128)} %bitcast.624) | dynamic-update-slice | bytes 3692164 | tf_op jit(solution)/shard_map/transpose(jvp(vmap()))/scatter-add
  2771.4 290.8 %while.28 = (s32[]{:T(128)}, f32[2,1,641,1,736]{4,3,2,1,0:T(1,128)}, s32[2,5]{1,0:T(2,128)S(1)}, f32[2,1,641,1,720]{4,3,2,1,0:T(1,128)}, s32[]{:T(128)}, /*index=5*/s32[5]{0:T(128)S(1)}, s32[]{:T(128)}) while((s32[]{:T(128)}, f32[2,1,641,1,736]{4,3,2,1,0:T(1,128)}, s32[2,5]{1,0:T(2,128)S(1)}, f32[2,1,641,1,720]{4,3,2,1,0:T(1,128)}, s32[]{:T(128)}, ...), condition=%wide.while_cond.10, body=%wide.while_body.10.sunk | while | flops 923061 | bytes 9230659 | solution.py:65
  2784.2 132.6 %dynamic-update-slice.73 = f32[2,1,641,1,736]{4,3,2,1,0:T(1,128)} dynamic-update-slice(f32[2,1,641,1,736]{4,3,2,1,0:T(1,128)} %get-tuple-element.1678, f32[1,1,641,1,720]{4,3,2,1,0:T(1,128)S(1)} %broadcast_select_fusion.19, s32[]{:T(128)} %bitcast.630, s32[]{:T(128)} %constant.58.clone.1..sunk.1, s32[]{:T(128)} %constant.58.clone.1..sunk.1, s32[]{:T(128)} %constant.58.clone.1..sunk.1, s32[]{:T(128)} %bitcast.631) | dynamic-update-slice | bytes 3692164 | tf_op jit(solution)/shard_map/transpose(jvp(vmap()))/scatter-add
  2929.5 132.6 %dynamic-update-slice.73 = f32[2,1,641,1,736]{4,3,2,1,0:T(1,128)} dynamic-update-slice(f32[2,1,641,1,736]{4,3,2,1,0:T(1,128)} %get-tuple-element.1678, f32[1,1,641,1,720]{4,3,2,1,0:T(1,128)S(1)} %broadcast_select_fusion.19, s32[]{:T(128)} %bitcast.630, s32[]{:T(128)} %constant.58.clone.1..sunk.1, s32[]{:T(128)} %constant.58.clone.1..sunk.1, s32[]{:T(128)} %constant.58.clone.1..sunk.1, s32[]{:T(128)} %bitcast.631) | dynamic-update-slice | bytes 3692164 | tf_op jit(solution)/shard_map/transpose(jvp(vmap()))/scatter-add
  3070.4 9.3 add_any.85
  3079.7 223.0 %while.29 = (s32[]{:T(128)}, f32[2,1,641,1,736]{4,3,2,1,0:T(1,128)}, s32[2,5]{1,0:T(2,128)S(1)}, f32[2,1,641,1,720]{4,3,2,1,0:T(1,128)}, s32[]{:T(128)}, /*index=5*/s32[5]{0:T(128)S(1)}, s32[]{:T(128)}) while((s32[]{:T(128)}, f32[2,1,641,1,736]{4,3,2,1,0:T(1,128)}, s32[2,5]{1,0:T(2,128)S(1)}, f32[2,1,641,1,720]{4,3,2,1,0:T(1,128)}, s32[]{:T(128)}, ...), condition=%wide.while_cond.11, body=%wide.while_body.11.sunk | while | flops 923061 | bytes 9230659 | solution.py:65
  3092.7 132.6 %dynamic-update-slice.74 = f32[2,1,641,1,736]{4,3,2,1,0:T(1,128)} dynamic-update-slice(f32[2,1,641,1,736]{4,3,2,1,0:T(1,128)} %get-tuple-element.1699, f32[1,1,641,1,720]{4,3,2,1,0:T(1,128)S(1)} %broadcast_select_fusion.20, s32[]{:T(128)} %bitcast.637, s32[]{:T(128)} %constant.58.clone.1..sunk.2, s32[]{:T(128)} %constant.58.clone.1..sunk.2, s32[]{:T(128)} %constant.58.clone.1..sunk.2, s32[]{:T(128)} %bitcast.638) | dynamic-update-slice | bytes 3692164 | tf_op jit(solution)/shard_map/transpose(jvp(vmap()))/scatter-add
  3238.0 64.7 %dynamic-update-slice.74 = f32[2,1,641,1,736]{4,3,2,1,0:T(1,128)} dynamic-update-slice(f32[2,1,641,1,736]{4,3,2,1,0:T(1,128)} %get-tuple-element.1699, f32[1,1,641,1,720]{4,3,2,1,0:T(1,128)S(1)} %broadcast_select_fusion.20, s32[]{:T(128)} %bitcast.637, s32[]{:T(128)} %constant.58.clone.1..sunk.2, s32[]{:T(128)} %constant.58.clone.1..sunk.2, s32[]{:T(128)} %constant.58.clone.1..sunk.2, s32[]{:T(128)} %bitcast.638) | dynamic-update-slice | bytes 3692164 | tf_op jit(solution)/shard_map/transpose(jvp(vmap()))/scatter-add
  3332.9 113.4 %all-reduce.18 = (f32[]{:T(128)}, f32[1282]{0:T(1024)S(1)}, f32[1,641]{1,0:T(1,128)S(1)}, f32[1,641]{1,0:T(1,128)S(1)}, f32[9,641]{1,0:T(8,128)S(1)}, /*index=5*/f32[8,641]{1,0:T(8,128)S(1)}) all-reduce(f32[]{:T(128)S(6)} %sub.94, f32[1282]{0:T(1024)S(1)} %copy-done.69, ...), channel_id=1, replica_groups=mesh['member'=4,'lat'=8] {'member','lat'}, use_global_device_ids=true, to_apply=%region_5.6 | all-reduce | flops 13462 | bytes 107696 | tf_op jit(solution)/shard_map/psum | solution.py:221
  3457.1 95.1 %all-reduce.22.cloned.1.call-done = (f32[641,1282]{1,0:T(8,128)}, f32[1282,641]{0,1:T(8,128)}) async-done(((f32[641,1282]{1,0:T(8,128)}, f32[1282,641]{0,1:T(8,128)}), (f32[641,1282]{1,0:T(8,128)}, f32[1282,641]{0,1:T(8,128)})) %all-reduce.22.cloned.1.call-update) | async-done | bytes 6574112 | tf_op jit(solution)/shard_map/psum | solution.py:221
  3563.5 11.1 fusion.118
  (444 shorter events, 559.4 us)
Async XLA Ops:
  7.2 7.3 copy-start
  7.2 7.2 copy-start.47
  7.2 464.2 %all-gather.2.cloned.1.call-start = ((), (), s32[]{:S(2)}) async-start(), calls=%async_computation | async-start | bytes 19691520 | tf_op jit(solution)/shard_map/all_gather | solution.py:173
  11.7 5.3 copy-start.32
  17.2 6.0 copy-start.42
  18.8 87.9 %collective-permute-start.1 = (bf16[1,641,1,720]{3,1,2,0:T(8,128)(2,1)}, bf16[1,641,1,720]{3,1,2,0:T(8,128)(2,1)}, u32[]{:S(2)}, u32[]{:S(2)}) collective-permute-start(bf16[1,641,1,720]{3,1,2,0:T(8,128)(2,1)} %get-tuple-element.764), channel_id=1, source_target_pairs={{1,0},{2,1},{3,2},{4,3},{5,4},{6,5},{7,6},{9,8},{10,9},{11,10},{12... | collective-permute-start | bytes 2769128 | tf_op jit(solution)/shard_map/ppermute | solution.py:29
  20.1 88.0 %collective-permute-start = (bf16[1,641,1,720]{3,1,2,0:T(8,128)(2,1)}, bf16[1,641,1,720]{3,1,2,0:T(8,128)(2,1)S(1)}, u32[]{:S(2)}, u32[]{:S(2)}) collective-permute-start(bf16[1,641,1,720]{3,1,2,0:T(8,128)(2,1)} %get-tuple-element.763), channel_id=1, source_target_pairs={{0,1},{1,2},{2,3},{3,4},{4,5},{5,6},{6,7},{8,9},{9,10},{10,11},{11... | collective-permute-start | bytes 2769128 | tf_op jit(solution)/shard_map/ppermute | solution.py:28
  23.2 85.1 %copy-start.61 = (pred[2]{0:T(512)(128)(4,1)}, pred[2]{0:T(512)(128)(4,1)S(1)}, u32[]{:S(2)}) copy-start(pred[2]{0:T(512)(128)(4,1)S(1)} %iota_compare_fusion.1) | copy-start | bytes 10
  29.5 6.0 copy-start.76
  85.2 19.1 copy-start.34
  103.6 415.1 %copy-start.64 = (f32[2]{0:T(128)}, f32[2]{0:T(128)S(1)}, u32[]{:S(2)}) copy-start(f32[2]{0:T(128)S(1)} %compare_convert_fusion) | copy-start | bytes 28
  241.8 17.7 copy-start.30
  241.8 17.7 copy-start.40
  259.5 24.9 copy-start.13
  284.4 6.1 copy-start.27
  284.4 6.1 copy-start.21
  284.4 6.1 copy-start.66
  314.7 6.2 copy-start.72
  314.7 6.2 copy-start.73
  314.7 6.2 copy-start.74
  314.7 6.2 copy-start.75
  318.8 3233.4 %all-reduce.22.cloned.1.call-start = ((), (), s32[]{:S(2)}) async-start(), calls=%async_computation.1 | async-start | bytes 14598144 | tf_op jit(solution)/shard_map/psum | solution.py:221
  327.7 191.0 %copy-start.29 = (bf16[641,2,720]{2,1,0:T(2,128)(2,1)S(1)}, bf16[641,2,720]{2,1,0:T(2,128)(2,1)}, u32[]{:S(2)}) copy-start(bf16[641,2,720]{2,1,0:T(2,128)(2,1)} %param.25) | copy-start | bytes 5538244
  471.4 47.3 %copy-start.4 = (f32[1,641,1,2,720]{4,1,3,2,0:T(8,128)S(1)}, f32[1,641,1,2,720]{4,1,3,2,0:T(8,128)}, u32[]{:S(2)}) copy-start(f32[1,641,1,2,720]{4,1,3,2,0:T(8,128)} %copy-done.3) | copy-start | bytes 11076484
  523.6 28.0 copy-start.10
  587.4 10.0 copy-start.86
  1199.7 9.3 copy-start.79
  1500.0 5.7 copy-start.9
  1505.6 10.0 copy-start.83
  1806.4 12.1 copy-start.82
  2117.0 9.2 copy-start.81
  2419.8 9.1 slice-start
  2420.7 8.3 slice-start.1
  2429.7 20.7 copy-start.20
  2429.7 20.7 copy-start.28
  2450.5 5.3 copy-start.57
  2450.5 5.3 copy-start.56
  2450.5 5.3 copy-start.55
  2450.5 5.3 copy-start.54
  2450.5 5.3 copy-start.53
  2450.5 5.3 copy-start.52
  2455.9 12.3 copy-start.80
  2759.2 12.2 copy-start.78
  3070.4 9.3 copy-start.77
  3302.7 9.7 copy-start.51
  3302.7 9.7 copy-start.12
  3302.7 11.5 copy-start.19
  3307.1 15.5 collective-permute-start.3
  3308.4 14.2 collective-permute-start.2
  3451.1 110.3 %copy-start.50 = (f32[8,641]{1,0:T(8,128)S(1)}, f32[8,641]{1,0:T(8,128)}, u32[]{:S(2)}) copy-start(f32[8,641]{1,0:T(8,128)} %param.45) | copy-start | bytes 61540
  3451.1 111.0 %copy-start.45 = (f32[9,641]{1,0:T(8,128)S(1)}, f32[9,641]{1,0:T(8,128)}, u32[]{:S(2)}) copy-start(f32[9,641]{1,0:T(8,128)} %param.42) | copy-start | bytes 69232
  3451.2 111.0 %copy-start.46 = (f32[9,641]{1,0:T(8,128)S(1)}, f32[9,641]{1,0:T(8,128)}, u32[]{:S(2)}) copy-start(f32[9,641]{1,0:T(8,128)} %param.43) | copy-start | bytes 69232
  3451.2 111.7 %copy-start.70 = (f32[2,641]{1,0:T(2,128)S(1)}, f32[2,641]{1,0:T(2,128)}, u32[]{:S(2)}) copy-start(f32[2,641]{1,0:T(2,128)} %param.40) | copy-start | bytes 15388
  3451.2 111.7 %copy-start.71 = (f32[2,641]{1,0:T(2,128)S(1)}, f32[2,641]{1,0:T(2,128)}, u32[]{:S(2)}) copy-start(f32[2,641]{1,0:T(2,128)} %param.41) | copy-start | bytes 15388
  3454.0 107.5 %copy-start.41 = (f32[8,641]{1,0:T(8,128)S(1)}, f32[8,641]{1,0:T(8,128)}, u32[]{:S(2)}) copy-start(f32[8,641]{1,0:T(8,128)} %param.33) | copy-start | bytes 61540
  3454.0 107.5 %copy-start.49 = (f32[8,641]{1,0:T(8,128)S(1)}, f32[8,641]{1,0:T(8,128)}, u32[]{:S(2)}) copy-start(f32[8,641]{1,0:T(8,128)} %param.44) | copy-start | bytes 61540
  3454.0 108.2 %copy-start.35 = (f32[9,641]{1,0:T(8,128)S(1)}, f32[9,641]{1,0:T(8,128)}, u32[]{:S(2)}) copy-start(f32[9,641]{1,0:T(8,128)} %param.32) | copy-start | bytes 69232
  3454.0 108.9 %copy-start.48 = (f32[2,641]{1,0:T(2,128)S(1)}, f32[2,641]{1,0:T(2,128)}, u32[]{:S(2)}) copy-start(f32[2,641]{1,0:T(2,128)} %param.31) | copy-start | bytes 15388
  3563.5 11.1 copy-start.67
  3563.5 11.1 copy-start.68
  3563.5 11.7 copy-start.14
  3563.5 11.7 copy-start.15
  3563.5 12.8 copy-start.23
  3563.5 13.9 copy-start.24
  (31 other events, 106.8 us)
Sparse Core Ops, SparseCore 0:
  318.9 152.4 all-gather.1
  3317.2 235.0 all-reduce.21
where the time goes:
time: 3620 us; the launch traced here: 3590 us
  local copies, waits for them, and re-layouts  2750 us (76%)
  other arithmetic  324 us (9%)
  waiting for transfers between devices  239 us (7%)
  matrix products  131 us (4%)
  blocking collectives  113 us (3%)
    scatter-add x72, local copies, waits for them, and re-layouts  2390 us
    gather x54, local copies, waits for them, and re-layouts  159 us
    scatter-add x36, other arithmetic  158 us
    all_gather x1, waiting for transfers between devices, on_device(): everyone = lax.all_gather(predicted, 'member', axis=0, tiled=True)  144 us
    unnamed x201, local copies, waits for them, and re-layouts  140 us
    psum x1, blocking collectives, on_device(): lax.psum((grad_expand, grad_bias_in, grad_reduce, grad_gain, grad_out_bia...  113 us
    psum x1, waiting for transfers between devices, on_device(): lax.psum((grad_expand, grad_bias_in, grad_reduce, grad_gain, grad_out_bia...  95.1 us
  transfers between devices with their start and end apart: 6, of which 2 were waited for; matrix products, arithmetic and copies ran while one was open for 3% of the time, Pallas kernels for 0%

commit v1 on v0

v1 whole, which is shorter than its diff:
```python
import functools
import math

import jax
import jax.numpy as jnp
from jax import lax
from jax.experimental import pallas as pl
from jax.experimental.pallas import tpu as pltpu
from jax.sharding import Mesh, PartitionSpec as P

STEP = 10
BETA_ONE = 0.9
BETA_TWO = 0.95
ADAM_EPS = 1e-08
DECAY_RATE = 0.1
NORM_EPS = 1e-05
SMALL_RATE = 0.3
REACH = 8
f32 = jnp.float32
bf16 = jnp.bfloat16

NN = (((1,), (0,)), ((), ()))
NT = (((1,), (1,)), ((), ()))
TN = (((0,), (0,)), ((), ()))


def round_up(value, step):
    return -(-value // step) * step


def mm(a, b, dims=NN):
    return lax.dot_general(a, b, dims, preferred_element_type=f32)


class Sizes:
    def __init__(self, members, channels, hidden, noise, lon):
        self.m = members
        self.c = channels
        self.h = hidden
        self.k = noise
        self.lon = lon
        self.q = lon // members
        self.pr = round_up(self.q, 8)
        self.ext = round_up(self.pr + 2 * REACH, 16)
        self.pe = 2 * self.pr
        self.p = members * self.pe
        self.pt = round_up(self.p, 256)
        self.cp = round_up(channels + noise, 128)
        self.ct = self.cp // 128
        self.cr = round_up(channels, 16)
        self.hp = round_up(hidden, 128)
        self.hm = hidden // 1280 * 1280 if hidden > 1280 else hidden


def smem():
    return pl.BlockSpec(memory_space=pltpu.SMEM)


def vmem():
    return pl.BlockSpec(memory_space=pltpu.VMEM)


def column_blocks(width, step):
    return [(i, min(step, width - i)) for i in range(0, width, step)]


def norm_rows(values, channels, lanes):
    inside = lanes < channels
    values = jnp.where(inside, values, 0.0)
    mean = jnp.sum(values, axis=1, keepdims=True) * (1.0 / channels)
    centred = jnp.where(inside, values - mean, 0.0)
    spread = jnp.sum(centred * centred, axis=1, keepdims=True) * (1.0 / channels)
    return centred, lax.rsqrt(spread + NORM_EPS)


def gelu_parts(v):
    size = jnp.abs(v)
    t = 1.0 / (1.0 + (0.3275911 * math.sqrt(0.5)) * size)
    bell = jnp.exp(-0.5 * v * v)
    poly = t * (
        0.5 * 0.254829592
        + t * (-0.5 * 0.284496736 + t * (0.5 * 1.421413741 + t * (-0.5 * 1.453152027 + t * (0.5 * 1.061405429))))
    )
    tail = poly * bell
    cdf = jnp.where(v >= 0.0, 1.0 - tail, tail)
    return v * cdf, cdf + v * bell * (1.0 / math.sqrt(2.0 * math.pi))


def main_kernel(
    sz,
    height_ref,
    taps_ref,
    x_ref,
    prev_ref,
    next_ref,
    target_ref,
    expand_ref,
    bias_ref,
    reduce_ref,
    gain_ref,
    outbias_ref,
    filter_ref,
    noisemix_ref,
    grad_e_ref,
    grad_r_ref,
    bg_ref,
    gn_own_ref,
    gn_prev_ref,
    gn_next_ref,
    filter_grad_ref,
    mixing_grad_ref,
    outbias_grad_ref,
    biasin_grad_ref,
    loss_ref,
    n_ref,
    mx_ref,
    act_ref,
    dg_ref,
    pred_ref,
    tr_ref,
    gn_ref,
    fil_ref,
):
    height = height_ref[0]
    lanes = lax.broadcasted_iota(jnp.int32, (1, sz.cp), 1)
    inside = (lanes < sz.c).astype(f32)
    below_first = jnp.where(height == 2, 2, 3)
    sources = ((0, 1, below_first), (1, 2, 3))
    two_pr = sz.pe

    def forward(e, carry):
        def norm_store(values, row):
            centred, inv = norm_rows(values.astype(f32), sz.c, lanes)
            normed = (centred * inv * gain_ref[...]).astype(bf16).astype(f32)
            for ct in range(sz.ct):
                n_ref[e, row, ct] = normed[:, ct * 128 : (ct + 1) * 128]

        norm_store(prev_ref[e], 0)
        norm_store(x_ref[e, 0], 1)
        norm_store(x_ref[e, 1], 2)
        norm_store(next_ref[e], 3)

        def filter_tile(ct, c):
            for r in range(2):
                acc = jnp.zeros((sz.pr, 128), f32)
                for a in range(3):
                    for j in range(3):
                        tap = 3 * a + j
                        start = taps_ref[tap, r] + REACH
                        moved = n_ref[e, sources[r][a], ct, pl.ds(start, sz.pr), :]
                        acc = acc + filter_ref[ct, tap : tap + 1, :] * moved
                fil_ref[ct, r * sz.pr : (r + 1) * sz.pr, :] = acc
            return c

        lax.fori_loop(0, sz.ct, filter_tile, 0)
        last = (sz.ct - 1) * 128
        noise = jnp.concatenate(
            [x_ref[e, r].astype(f32)[REACH : REACH + sz.pr, last:] for r in range(2)], axis=0
        ).astype(bf16)
        mixed = mm(jnp.concatenate([noise, noise], axis=1), noisemix_ref[...])
        filtered = jnp.concatenate([fil_ref[ct] for ct in range(sz.ct)], axis=1)
        mixed = (filtered + mixed).astype(bf16)
        rows = pl.ds(pl.multiple_of(e * two_pr, 16), two_pr)
        mx_ref[rows, :] = mixed
        for at, width in column_blocks(sz.hp, 256):
            pre = mm(mixed, expand_ref[:, at : at + width]) + bias_ref[:, at : at + width]
            act, slope = gelu_parts(pre)
            act_ref[rows, at : at + width] = act.astype(bf16)
            dg_ref[rows, at : at + width] = slope.astype(bf16)
        branch = mm(act_ref[rows, :], reduce_ref[...], NT) + outbias_ref[...]
        own = jnp.concatenate([x_ref[e, r].astype(f32)[REACH : REACH + sz.pr] for r in range(2)], axis=0)
        pred_ref[e] = own + branch
        return carry

    lax.fori_loop(0, sz.m, forward, 0)

    loss_ref[...] = jnp.zeros_like(loss_ref)
    outbias_grad_ref[...] = jnp.zeros_like(outbias_grad_ref)
    step = 16
    inv_m = 1.0 / sz.m
    inv_mm = inv_m * inv_m

    def score(i, carry):
        at = pl.multiple_of(i * step, step)
        pixel = at + lax.broadcasted_iota(jnp.int32, (step, 1), 0)
        row = (pixel >= sz.pr).astype(jnp.int32)
        use = (pixel - row * sz.pr < sz.q) & (row < height)
        mask_rows = use.astype(f32)
        for ct in range(sz.ct):
            cols = slice(ct * 128, (ct + 1) * 128)
            mask = mask_rows * inside[:, cols]
            preds = [pred_ref[e, pl.ds(at, step), cols] for e in range(sz.m)]
            truth = target_ref[pl.ds(at, step), cols].astype(f32)
            slopes = []
            own_sum = 0.0
            for p in preds:
                d = p - truth
                q = d * d + 1.0
                r = lax.rsqrt(q)
                own_sum = own_sum + q * r
                slopes.append(d * r * inv_m)
            pair_sum = 0.0
            pairs = [0.0] * sz.m
            for a in range(sz.m):
                for b in range(a + 1, sz.m):
                    d = preds[a] - preds[b]
                    q = d * d + 1.0
                    r = lax.rsqrt(q)
                    pair_sum = pair_sum + q * r
                    s = d * r
                    pairs[a] = pairs[a] + s
                    pairs[b] = pairs[b] - s
            value = own_sum * inv_m - (pair_sum + 0.5 * sz.m) * inv_mm
            loss_ref[...] += mask * value
            total = 0.0
            for e in range(sz.m):
                g = (mask * (slopes[e] - pairs[e] * inv_mm)).astype(bf16)
                where = pl.ds(pl.multiple_of(e * two_pr + at, 16), step)
                bg_ref[where, cols] = g
                total = total + g.astype(f32)
            outbias_grad_ref[:, cols] += total[0:8] + total[8:16]
        return carry

    lax.fori_loop(0, two_pr // step, score, 0)
    if sz.pt > sz.p:
        bg_ref[sz.p :, :] = jnp.zeros((sz.pt - sz.p, sz.cp), bf16)
        mx_ref[sz.p :, :] = jnp.zeros((sz.pt - sz.p, sz.cp), bf16)
        act_ref[sz.p :, :] = jnp.zeros((sz.pt - sz.p, sz.hp), bf16)

    def transpose_into(src):
        def body(i, c):
            at = pl.ds(pl.multiple_of(i * 128, 128), 128)
            for ct in range(sz.ct):
                block = src[at, ct * 128 : (ct + 1) * 128].astype(f32).T.astype(bf16)
                size = min(128, sz.cr - ct * 128)
                if size > 0:
                    tr_ref[ct * 128 : ct * 128 + size, at] = block[:size]
            return c

        lax.fori_loop(0, sz.pt // 128, body, 0)

    transpose_into(bg_ref)
    for at, width in column_blocks(sz.hp, 256):
        grad_r_ref[:, at : at + width] = mm(tr_ref[...], act_ref[:, at : at + width]).astype(bf16)

    gn_ref[...] = jnp.zeros_like(gn_ref)
    filter_grad_ref[...] = jnp.zeros_like(filter_grad_ref)
    biasin_grad_ref[...] = jnp.zeros_like(biasin_grad_ref)
    mixing_grad_ref[...] = jnp.zeros_like(mixing_grad_ref)

    def backward(e, carry):
        rows = pl.ds(pl.multiple_of(e * two_pr, 16), two_pr)
        bg = bg_ref[rows, :]
        for at, width in column_blocks(sz.hp, 256):
            grad = mm(bg, reduce_ref[:, at : at + width])
            pre = (grad * dg_ref[rows, at : at + width].astype(f32)).astype(bf16)
            act_ref[rows, at : at + width] = pre
            wide = pre.astype(f32)
            biasin_grad_ref[:, at : at + width] += jnp.sum(wide.reshape(-1, 8, width), axis=0)
        gm = mm(act_ref[rows, :], expand_ref[...], NT)
        for ct in range(sz.ct):
            fil_ref[ct] = gm[:, ct * 128 : (ct + 1) * 128]
        last = (sz.ct - 1) * 128
        noise = jnp.concatenate(
            [x_ref[e, r].astype(f32)[REACH : REACH + sz.pr, last:] for r in range(2)], axis=0
        )
        mixing_grad_ref[...] += mm(noise.T[0:16].astype(bf16), gm.astype(bf16))

        def unfilter_tile(ct, c):
            for r in range(2):
                g = fil_ref[ct, r * sz.pr : (r + 1) * sz.pr, :]
                for a in range(3):
                    source = sources[r][a]
                    for j in range(3):
                        tap = 3 * a + j
                        where = pl.ds(taps_ref[tap, r] + REACH, sz.pr)
                        gn_ref[e, source, ct, where, :] += filter_ref[ct, tap : tap + 1, :] * g
                        product = g * n_ref[e, source, ct, where, :]
                        filter_grad_ref[ct, tap] += jnp.sum(product.reshape(-1, 8, 128), axis=0)
            return c

        lax.fori_loop(0, sz.ct, unfilter_tile, 0)
        for ct in range(sz.ct):
            cols = slice(ct * 128, (ct + 1) * 128)
            gn_prev_ref[e, :, cols] = gn_ref[e, 0, ct].astype(bf16)
            gn_next_ref[e, :, cols] = gn_ref[e, 3, ct].astype(bf16)
            gn_own_ref[e, 0, :, cols] = gn_ref[e, 1, ct]
            gn_own_ref[e, 1, :, cols] = gn_ref[e, 2, ct]
        return carry

    lax.fori_loop(0, sz.m, backward, 0)
    transpose_into(mx_ref)
    for at, width in column_blocks(sz.hp, 256):
        grad_e_ref[:, at : at + width] = mm(tr_ref[...], act_ref[:, at : at + width]).astype(bf16)


def main_call(sz, height, taps, x, prev, after, target, expand, bias, reduce, gain, outbias, filt, noisemix):
    shape = jax.ShapeDtypeStruct
    outs = (
        shape((sz.cr, sz.hp), bf16),
        shape((sz.cr, sz.hp), bf16),
        shape((sz.pt, sz.cp), bf16),
        shape((sz.m, 2, sz.ext, sz.cp), f32),
        shape((sz.m, sz.ext, sz.cp), bf16),
        shape((sz.m, sz.ext, sz.cp), bf16),
        shape((sz.ct, 9, 8, 128), f32),
        shape((16, sz.cp), f32),
        shape((8, sz.cp), f32),
        shape((8, sz.hp), f32),
        shape((16, 128), f32),
    )
    return pl.pallas_call(
        functools.partial(main_kernel, sz),
        out_shape=outs,
        in_specs=[smem(), smem()] + [vmem()] * 11,
        out_specs=tuple(vmem() for _ in outs),
        scratch_shapes=[
            pltpu.VMEM((sz.m, 4, sz.ct, sz.ext, 128), f32),
            pltpu.VMEM((sz.pt, sz.cp), bf16),
            pltpu.VMEM((sz.pt, sz.hp), bf16),
            pltpu.VMEM((sz.p, sz.hp), bf16),
            pltpu.VMEM((sz.m, sz.pe, sz.cp), f32),
            pltpu.VMEM((sz.cr, sz.pt), bf16),
            pltpu.VMEM((sz.m, 4, sz.ct, sz.ext, 128), f32),
            pltpu.VMEM((sz.ct, sz.pe, 128), f32),
        ],
        compiler_params=pltpu.CompilerParams(vmem_limit_bytes=63 * 1024 * 1024),
        name="main",
    )(height, taps, x, prev, after, target, expand, bias, reduce, gain, outbias, filt, noisemix)


def norm_back_kernel(sz, height_ref, x_ref, gn_ref, up_ref, down_ref, bg_ref, gain_ref, out_ref, gain_grad_ref):
    height = height_ref[0]
    lanes = lax.broadcasted_iota(jnp.int32, (1, sz.cp), 1)
    gain_grad_ref[...] = jnp.zeros_like(gain_grad_ref)

    def body(e, carry):
        from_up = up_ref[e].astype(f32)
        from_down = down_ref[e].astype(f32)
        rows = pl.ds(pl.multiple_of(e * sz.pe, 16), sz.pe)
        direct = bg_ref[rows, :].astype(f32)
        for r in range(2):
            centred, inv = norm_rows(x_ref[e, r].astype(f32), sz.c, lanes)
            xhat = centred * inv
            g = gn_ref[e, r] + jnp.where(height == r + 1, from_down, 0.0)
            if r == 0:
                g = g + from_up
            gain_grad_ref[...] += jnp.sum((g * xhat).reshape(-1, 8, sz.cp), axis=0)
            q = g * gain_ref[...]
            mean_q = jnp.sum(q, axis=1, keepdims=True) * (1.0 / sz.c)
            mean_qx = jnp.sum(q * xhat, axis=1, keepdims=True) * (1.0 / sz.c)
            result = (q - mean_q - xhat * mean_qx) * inv
            out_ref[e, r] = result.astype(bf16)
            part = result[REACH : REACH + sz.pr] + direct[r * sz.pr : (r + 1) * sz.pr]
            pieces = [result[:REACH], part, result[REACH + sz.pr :]]
            out_ref[e, r] = jnp.concatenate(pieces, axis=0).astype(bf16)
        return carry

    lax.fori_loop(0, sz.m, body, 0)


def norm_back_call(sz, height, x, gn, up, down, bg, gain):
    shape = jax.ShapeDtypeStruct
    outs = (shape((sz.m, 2, sz.ext, sz.cp), bf16), shape((8, sz.cp), f32))
    return pl.pallas_call(
        functools.partial(norm_back_kernel, sz),
        out_shape=outs,
        in_specs=[smem()] + [vmem()] * 6,
        out_specs=tuple(vmem() for _ in outs),
        compiler_params=pltpu.CompilerParams(vmem_limit_bytes=40 * 1024 * 1024),
        name="norm_back",
    )(height, x, gn, up, down, bg, gain)


def exchange(pieces, axis, count):
    result = [pieces[0]]
    for s in range(1, count):
        result.append(lax.ppermute(pieces[s], axis, [(i, i ^ s) for i in range(count)]))
    return result


def reduce_over(values, axis, count, dim):
    me = lax.axis_index(axis)
    size = values.shape[dim] // count
    pieces = [lax.dynamic_slice_in_dim(values, (me ^ s) * size, size, axis=dim) for s in range(count)]
    arrived = exchange(pieces, axis, count)
    return sum(part.astype(f32) for part in arrived)


def gather_over(values, axis, count, dim):
    me = lax.axis_index(axis)
    stacked = jnp.stack(exchange([values] * count, axis, count))
    ordered = [lax.dynamic_index_in_dim(stacked, me ^ k, 0, keepdims=False) for k in range(count)]
    return jnp.concatenate(ordered, axis=dim)


def adam_step(weight, gradient, first, second, rate):
    first_new = BETA_ONE * first + (1.0 - BETA_ONE) * gradient
    second_new = BETA_TWO * second + (1.0 - BETA_TWO) * gradient * gradient
    first_hat = first_new / (1.0 - BETA_ONE**STEP)
    second_hat = second_new / (1.0 - BETA_TWO**STEP)
    weight_new = weight - rate * (
        first_hat / (jnp.sqrt(second_hat) + ADAM_EPS) + DECAY_RATE * weight
    )
    return (weight_new, first_new, second_new)


def pad_to(values, shape):
    return jnp.pad(values, [(0, n - m) for n, m in zip(shape, values.shape)])


def on_device(
    fields,
    noise_fields,
    target_fields,
    band_heights,
    tap_offsets,
    expand_weight,
    expand_bias,
    reduce_weight,
    channel_vectors,
    disco_filter,
    noise_mixing,
    first_expand,
    second_expand,
    first_bias,
    second_bias,
    first_reduce,
    second_reduce,
    first_vectors,
    second_vectors,
    first_filter,
    second_filter,
    first_mixing,
    second_mixing,
):
    members = lax.axis_size("member")
    stacks = lax.axis_size("stack")
    lat_count = 2 * stacks
    lat = ("stack", "core")
    channels, hidden = expand_weight.shape
    lon = fields.shape[3]
    sz = Sizes(members, channels, hidden, noise_fields.shape[1], lon)
    me = lax.axis_index("member")
    core = lax.axis_index("core")
    band = lax.axis_index("stack") * 2 + core
    height = lax.dynamic_slice_in_dim(band_heights, band, 1)

    both = jnp.concatenate([fields[0], noise_fields[0]], axis=0)
    both = jnp.transpose(both, (1, 2, 0))
    both = pad_to(both, (2, lon, sz.cp))
    tail = sz.ext - REACH - sz.q
    around = jnp.concatenate([both[:, lon - REACH :], both, both[:, :tail]], axis=1)
    pieces = [lax.dynamic_slice_in_dim(around, (me ^ s) * sz.q, sz.ext, axis=1) for s in range(members)]
    x = jnp.stack(exchange(pieces, "member", members))
    upward = [(i, i + 1) for i in range(lat_count - 1)]
    downward = [(i + 1, i) for i in range(lat_count - 1)]
    bottom = lax.dynamic_index_in_dim(x, height[0] - 1, 1, keepdims=False)
    prev = lax.ppermute(bottom, lat, upward)
    after = lax.ppermute(x[:, 0], lat, downward)

    truth = pad_to(target_fields, (channels, 2, lon + sz.pr - sz.q))
    truth = lax.dynamic_slice_in_dim(truth, me * sz.q, sz.pr, axis=2)
    truth = pad_to(jnp.transpose(truth, (1, 2, 0)), (2, sz.pr, sz.cp)).reshape(sz.pe, sz.cp)

    expand_low = pad_to(expand_weight.astype(bf16), (sz.cp, sz.hp))
    reduce_low = pad_to(reduce_weight.T.astype(bf16), (sz.cp, sz.hp))
    bias = pad_to(expand_bias[None], (1, sz.hp))
    gain = pad_to(channel_vectors[0:1], (1, sz.cp))
    outbias = pad_to(channel_vectors[1:2], (1, sz.cp))
    filt = jnp.transpose(pad_to(disco_filter, (16, sz.cp)).reshape(16, sz.ct, 128), (1, 0, 2))
    at = channels - (sz.ct - 1) * 128
    coarse = noise_mixing.astype(bf16)
    fine = (noise_mixing - coarse.astype(f32)).astype(bf16)
    noisemix = jnp.zeros((256, sz.cp), bf16)
    noisemix = noisemix.at[at : at + sz.k, :channels].set(coarse)
    noisemix = noisemix.at[128 + at : 128 + at + sz.k, :channels].set(fine)

    (
        grad_e,
        grad_r,
        bg,
        gn_own,
        gn_prev,
        gn_next,
        filter_part,
        mixing_part,
        outbias_part,
        biasin_part,
        loss_part,
    ) = main_call(
        sz, height, tap_offsets, x, prev, after, truth, expand_low, bias, reduce_low, gain, outbias, filt, noisemix
    )

    up = lax.ppermute(gn_next, lat, upward)
    down = lax.ppermute(gn_prev, lat, downward)
    own_grad, gain_part = norm_back_call(sz, height, x, gn_own, up, down, bg, gain)

    returned = jnp.stack(exchange([own_grad[s] for s in range(members)], "member", members))
    parts = [lax.dynamic_index_in_dim(returned, me ^ j, 0, keepdims=False) for j in range(members)]
    total = jnp.zeros((2, lon, channels), f32)
    lefts, mids, rights = [], [], []
    for part in parts:
        wide = part[:, :, :channels].astype(f32)
        lefts.append(wide[:, :REACH])
        mids.append(wide[:, REACH : REACH + sz.q])
        rights.append(wide[:, REACH + sz.q : 2 * REACH + sz.q])
    rows = []
    for j in range(members):
        extra = jnp.concatenate(
            [rights[j - 1], jnp.zeros((2, sz.q - 2 * REACH, channels), f32), lefts[(j + 1) % members]], axis=1
        )
        rows.append(mids[j] + extra)
    total = jnp.concatenate(rows, axis=1).astype(bf16)
    input_gradient = jnp.transpose(total, (2, 0, 1))[None]

    main_c = channels // (4 * 16 * 2) * (4 * 16 * 2)
    main_h = hidden // 256 * 256
    grads = jnp.stack([grad_e[:main_c, :main_h], grad_r[:main_c, :main_h]])
    half = main_h // 2
    mine = lax.dynamic_slice_in_dim(grads, core * half, half, axis=2)
    other = lax.dynamic_slice_in_dim(grads, (1 - core) * half, half, axis=2)
    swap = [(0, 1), (1, 0)]
    got = lax.ppermute(other, "core", swap)
    part = (mine.astype(f32) + got.astype(f32)).astype(bf16)
    part = reduce_over(part, "member", members, 1).astype(bf16)
    part = reduce_over(part, "stack", stacks, 1).astype(bf16)
    part = gather_over(part, "stack", stacks, 1)
    part = gather_over(part, "member", members, 1)
    got = lax.ppermute(part, "core", swap)
    low_half = jnp.where(core == 0, part, got)
    high_half = jnp.where(core == 0, got, part)
    grads = jnp.concatenate([low_half, high_half], axis=2)

    filter_rows = jnp.transpose(jnp.sum(filter_part, axis=2), (1, 0, 2)).reshape(9, sz.cp)
    small_parts = [
        filter_rows[:, :channels],
        mixing_part[at : at + sz.k, :channels],
        jnp.sum(gain_part, axis=0)[:channels],
        jnp.sum(outbias_part, axis=0)[:channels],
        jnp.sum(biasin_part, axis=0)[:hidden],
        grad_e[main_c:channels, :hidden].astype(f32),
        grad_r[main_c:channels, :hidden].astype(f32),
        grad_e[:main_c, main_h:hidden].astype(f32),
        grad_r[:main_c, main_h:hidden].astype(f32),
        jnp.sum(loss_part),
    ]
    flat = jnp.concatenate([v.reshape(-1) for v in small_parts])
    width = round_up(flat.shape[0], 1024)
    flat = jnp.pad(flat, (0, width - flat.shape[0])).reshape(-1, 128)
    flat = flat + lax.ppermute(flat, "core", swap)
    flat = sum(exchange([flat] * members, "member", members))
    flat = sum(exchange([flat] * stacks, "stack", stacks))
    flat = flat.reshape(-1)
    summed = []
    offset = 0
    for v in small_parts:
        summed.append(flat[offset : offset + v.size].reshape(v.shape))
        offset += v.size
    (
        sum_filter,
        sum_mixing,
        sum_gain,
        sum_bias_out,
        sum_bias_in,
        row_e,
        row_r,
        col_e,
        col_r,
        loss_total,
    ) = summed

    def whole(main, row, col):
        return jnp.concatenate([jnp.concatenate([main.astype(f32), col], axis=1), row], axis=0)

    sum_expand = whole(grads[0], row_e, col_e)
    sum_reduce = whole(grads[1], row_r, col_r)
    sum_vectors = jnp.stack([sum_gain, sum_bias_out])
    live_total = jnp.sum(band_heights).astype(f32)
    mean_loss = loss_total / (channels * lon * live_total)
    squares = (
        jnp.sum(sum_expand * sum_expand)
        + jnp.sum(sum_bias_in * sum_bias_in)
        + jnp.sum(sum_reduce * sum_reduce)
        + jnp.sum(sum_vectors * sum_vectors)
        + jnp.sum(sum_filter * sum_filter)
        + jnp.sum(sum_mixing * sum_mixing)
    )
    gradient_norm = jnp.sqrt(squares)
    limit = 0.02 * math.sqrt(hidden * channels * lat_count * 2 * lon / members)
    factor = jnp.minimum(1.0, limit / (gradient_norm + 1e-06))
    expand_out, expand_first, expand_second = adam_step(
        expand_weight, factor * sum_expand, first_expand, second_expand, channels ** (-0.5)
    )
    bias_out, bias_first, bias_second = adam_step(
        expand_bias, factor * sum_bias_in, first_bias, second_bias, SMALL_RATE
    )
    reduce_out, reduce_first, reduce_second = adam_step(
        reduce_weight.T, factor * sum_reduce, first_reduce.T, second_reduce.T, hidden ** (-0.5)
    )
    vectors_out, vectors_first, vectors_second = adam_step(
        channel_vectors, factor * sum_vectors, first_vectors, second_vectors, SMALL_RATE
    )
    filter_out, filter_first, filter_second = adam_step(
        disco_filter, factor * sum_filter, first_filter, second_filter, SMALL_RATE
    )
    mixing_out, mixing_first, mixing_second = adam_step(
        noise_mixing, factor * sum_mixing, first_mixing, second_mixing, SMALL_RATE
    )
    return (
        mean_loss,
        input_gradient,
        gradient_norm,
        expand_out,
        expand_first,
        expand_second,
        bias_out,
        bias_first,
        bias_second,
        reduce_out.T,
        reduce_first.T,
        reduce_second.T,
        vectors_out,
        vectors_first,
        vectors_second,
        filter_out,
        filter_first,
        filter_second,
        mixing_out,
        mixing_first,
        mixing_second,
        expand_out.astype(bf16),
        reduce_out.astype(bf16).T,
    )


def solution(mesh):
    members = mesh.shape["member"]
    lat = mesh.shape["lat"]
    split = Mesh(mesh.devices.reshape(members, lat // 2, 2), ("member", "stack", "core"))
    rows = ("stack", "core")
    whole = [P()] * 18
    in_specs = (
        P("member", None, rows, None),
        P("member", None, rows, None),
        P(None, rows, None),
        P(),
        P(None, rows),
        *whole,
    )
    out_specs = (P(), P("member", None, rows, None)) + (P(),) * 21
    return jax.shard_map(on_device, mesh=split, in_specs=in_specs, out_specs=out_specs, check_vma=False)
```

time: 3620 us -> 322 us (0.09)
  local copies, waits for them, and re-layouts: 2750 us -> 48 us
  other arithmetic: 324 us -> 55.4 us
  waiting for transfers between devices: 239 us -> 87.7 us
  matrix products: 131 us -> 0 us
  blocking collectives: 113 us -> 0 us
  Pallas kernels: 0 us -> 68.4 us
  starting transfers between devices: 9.94 us -> 50.7 us
    scatter-add x75 -> x0, local copies, waits for them, and re-layouts: 2400 us -> none
    gather x54 -> x0, local copies, waits for them, and re-layouts: 159 us -> none
    scatter-add x37 -> x0, other arithmetic: 159 us -> none
    all_gather x1 -> x0, waiting for transfers between devices: 144 us -> none  [on_device(): everyone = lax.all_gather(predicted, 'member', axis=0, tiled=True)]
    dot_general x8 -> x0, matrix products: 131 us -> none  [the longest x1 28 us: on_device(): jnp.einsum('hc,ecgrl->ehgrl', reduce_low, branch_grad, preferred_element_...]
    unnamed x201 -> x89, local copies, waits for them, and re-layouts: 140 us -> 22.6 us
    psum x1 -> x0, blocking collectives: 113 us -> none  [on_device(): lax.psum((grad_expand, grad_bias_in, grad_reduce, grad_gain, grad_out_bia...]
    psum x1 -> x0, waiting for transfers between devices: 95.1 us -> none  [on_device(): lax.psum((grad_expand, grad_bias_in, grad_reduce, grad_gain, grad_out_bia...]
  transfers between devices with their start and end apart: 6 -> 31, of which waited for: 2 -> 15; matrix products, arithmetic and copies ran while one was open for 3% -> 15% of each run, Pallas kernels for 0% -> 0%
where the time goes in v1:
time: 322 us; the launch traced here: 320 us
  waiting for transfers between devices  87.7 us (27%)
  Pallas kernels  68.4 us (21%)
  other arithmetic  55.4 us (17%)
  starting transfers between devices  50.7 us (16%)
  local copies, waits for them, and re-layouts  48 us (15%)
  between operations  10.3 us (3%)
    ppermute x24, waiting for transfers between devices, exchange(): lax.ppermute(pieces[s], axis, [(i, i ^ s) for i in range(count)])  87.7 us
    pallas_call x1, Pallas kernels, main_call(): pl.pallas_call(functools.partial(main_kernel, sz), out_shape=outs, in_spe...  60.8 us
    ppermute x24, starting transfers between devices, exchange(): lax.ppermute(pieces[s], axis, [(i, i ^ s) for i in range(count)])  33.3 us
    unnamed x89, local copies, waits for them, and re-layouts  22.6 us
    convert_element_type x1, other arithmetic, on_device(): expand_out.astype(bf16)  11.8 us
    pallas_call x1, Pallas kernels, norm_back_call(): pl.pallas_call(functools.partial(norm_back_kernel, sz), out_shape=outs, i...  7.56 us
    pad x7, local copies, waits for them, and re-layouts, pad_to(): return jnp.pad(values, [(0, n - m) for n, m in zip(shape, values.shape)])  7.2 us
    transpose x1, other arithmetic, on_device(): reduce_out.astype(bf16)  6.84 us
  transfers between devices with their start and end apart: 31, of which 15 were waited for; matrix products, arithmetic and copies ran while one was open for 15% of the time, Pallas kernels for 0%

profile of v1, /device:TPU:0, one launch (start us, length us, event | category | flops | bytes accessed | tf_op | source)
XLA Modules:
  0.0 320.5 jit_solution(509551560624447420)
XLA Ops:
  1.6 6.6 %copy.56 = bf16[1,641,2,720]{1,3,2,0:T(8,128)(2,1)} copy(bf16[1,641,2,720]{3,2,1,0:T(2,128)(2,1)} %param.27) | data formatting | bytes 3692160 | tf_op args[0]
  8.2 1.9 maximum_bitcast_fusion
  10.2 1.6 pad.47
  11.8 1.8 pad_maximum_fusion.4
  14.2 3.9 %collective-permute-start.2 = (bf16[2,208,768]{2,1,0:T(8,128)(2,1)S(1)}, bf16[2,208,768]{2,1,0:T(8,128)(2,1)S(1)}, u32[]{:S(2)}, u32[]{:S(2)}) collective-permute-start(bf16[2,208,768]{2,1,0:T(8,128)(2,1)S(1)} %get-tuple-element.156), channel_id=1, source_target_pairs={{0,24},{8,16},{16,8},{24,0},{1,25},{9,17},{17,9},{25,1},{2,26},{10... | collective-permute-start | bytes 1916936 | tf_op jit(solution)/shard_map/ppermute | solution.py:378
  20.7 12.7 %collective-permute-done.2 = bf16[2,208,768]{2,1,0:T(8,128)(2,1)S(1)} collective-permute-done((bf16[2,208,768]{2,1,0:T(8,128)(2,1)S(1)}, bf16[2,208,768]{2,1,0:T(8,128)(2,1)S(1)}, u32[]{:S(2)}, u32[]{:S(2)}) %collective-permute-start.2) | collective-permute-done | bytes 639008 | tf_op jit(solution)/shard_map/ppermute | solution.py:378
  33.4 12.9 %collective-permute-done.1 = bf16[2,208,768]{2,1,0:T(8,128)(2,1)} collective-permute-done((bf16[2,208,768]{2,1,0:T(8,128)(2,1)S(1)}, bf16[2,208,768]{2,1,0:T(8,128)(2,1)}, u32[]{:S(2)}, u32[]{:S(2)}) %collective-permute-start.1) | collective-permute-done | bytes 639008 | tf_op jit(solution)/shard_map/ppermute | solution.py:378
  46.6 1.6 pad_maximum_fusion.2.x_ref
  48.3 1.2 slice_bitcast_fusion.2
  50.2 2.8 collective-permute-start.3
  53.0 1.3 collective-permute-start.4
  54.3 1.5 fusion.15
  58.3 2.2 convert_element_type.110
  60.5 1.5 pad.50.expand_ref
  62.0 1.3 copy-done.11
  63.5 1.5 pad.52.reduce_ref
  68.1 60.8 %main.1 = (bf16[656,1408]{1,0:T(8,128)(2,1)}, bf16[656,1408]{1,0:T(8,128)(2,1)}, bf16[1536,768]{1,0:T(8,128)(2,1)}, f32[4,2,208,768]{3,2,1,0:T(8,128)}, bf16[4,2...) custom-call(s32[1]{0:T(128)} %dynamic_slice.91.height_ref, ...), custom_call_target="tpu_custom_call" | custom-call | tf_op jit(solution)/shard_map/main/pallas_call | solution.py:312
  129.0 6.7 %collective-permute-start.5 = (bf16[4,208,768]{2,1,0:T(8,128)(2,1)}, bf16[4,208,768]{2,1,0:T(8,128)(2,1)S(1)}, u32[]{:S(2)}, u32[]{:S(2)}) collective-permute-start(bf16[4,208,768]{2,1,0:T(8,128)(2,1)} %get-tuple-element.63), channel_id=1, source_target_pairs={{0,1},{1,2},{2,3},{3,4},{4,5},{5,6},{6,7},{8,9},{9,10},{10,11},{11... | collective-permute-start | bytes 3833864 | tf_op jit(solution)/shard_map/ppermute | solution.py:495
  135.7 1.3 collective-permute-start.6
  140.6 1.0 slice_convert_fusion.4
  142.0 1.3 reduce_sum.112
  144.2 4.0 %slice_bitcast_fusion = (bf16[1,640,1280]{2,1,0:T(8,128)(2,1)}, bf16[1,640,1280]{2,1,0:T(8,128)(2,1)}) fusion(bf16[656,1408]{1,0:T(8,128)(2,1)} %get-tuple-element.70, bf16[656,1408]{1,0:T(8,128)(2,1)} %get-tuple-element.69), kind=kLoop, calls=%fused_computation.40 | loop fusion | bytes 6553600 | tf_op jit(solution)/shard_map/stack | solution.py:519
  148.2 1.0 copy-done.3
  149.2 1.0 copy-done.5
  150.3 1.3 copy-done.4
  151.6 1.3 copy-done.6
  152.9 7.6 %norm_back.1 = (bf16[4,2,208,768]{3,2,1,0:T(8,128)(2,1)S(1)}, f32[8,768]{1,0:T(8,128)S(1)}) custom-call(s32[1]{0:T(128)} %dynamic_slice.91.height_ref, bf16[4,2,208,768]{3,2,1,0:T(8,128)(2,1)S(1)} %copy-done.1, f32[4,2,208,768]{3,2,1,0:T(8,128)} %get-tuple-element.62.gn_ref, bf16[4,208,768]{2,1,0:T(8,128)(2,1)S(1)} %copy-done.4, ...), custom_call_target="tpu_custom_call" | custom-call | tf_op jit(solution)/shard_map/norm_back/pallas_call | solution.py:365
  161.2 5.2 %collective-permute-start.7 = (f32[152,128]{1,0:T(8,128)S(1)}, f32[152,128]{1,0:T(8,128)S(1)}, u32[]{:S(2)}, u32[]{:S(2)}) collective-permute-start(f32[152,128]{1,0:T(8,128)S(1)} %pad_bitcast_fusion), channel_id=1, source_target_pairs={{0,1},{1,0},{2,3},{3,2},{4,5},{5,4},{6,7},{7,6},{8,9},{9,8},{10,11... | collective-permute-start | bytes 233480 | tf_op jit(solution)/shard_map/ppermute | solution.py:551
  166.5 2.7 fusion.7
  169.2 1.7 collective-permute-start.10
  171.0 1.3 collective-permute-start.9
  175.0 1.6 collective-permute-done.9
  176.7 2.5 collective-permute-start.13
  179.8 1.3 collective-permute-start.11
  181.1 1.3 fusion.30
  182.4 1.6 collective-permute-start.16
  184.1 1.3 collective-permute-start.15
  185.4 1.7 collective-permute-done.12
  188.4 1.9 add_convert_fusion
  191.2 1.7 collective-permute-start.20
  192.8 1.3 collective-permute-start.19
  198.7 11.1 %collective-permute-done.20 = bf16[2,160,640]{2,1,0:T(8,128)(2,1)} collective-permute-done((bf16[2,160,640]{2,1,0:T(8,128)(2,1)}, bf16[2,160,640]{2,1,0:T(8,128)(2,1)}, u32[]{:S(2)}, u32[]{:S(2)}) %collective-permute-start.20) | collective-permute-done | bytes 409632 | tf_op jit(solution)/shard_map/ppermute | solution.py:378
  209.8 1.5 collective-permute-start.14
  211.2 19.1 %collective-permute-done.19 = bf16[2,160,640]{2,1,0:T(8,128)(2,1)} collective-permute-done((bf16[2,160,640]{2,1,0:T(8,128)(2,1)S(1)}, bf16[2,160,640]{2,1,0:T(8,128)(2,1)}, u32[]{:S(2)}, u32[]{:S(2)}) %collective-permute-start.19) | collective-permute-done | bytes 409632 | tf_op jit(solution)/shard_map/ppermute | solution.py:378
  230.3 1.5 add_convert_fusion.1
  231.9 1.9 collective-permute-start.23
  234.7 4.9 %collective-permute-done.23 = bf16[2,40,640]{2,1,0:T(8,128)(2,1)S(1)} collective-permute-done((bf16[2,40,640]{2,1,0:T(8,128)(2,1)S(1)}, bf16[2,40,640]{2,1,0:T(8,128)(2,1)S(1)}, u32[]{:S(2)}, u32[]{:S(2)}) %collective-permute-start.23) | collective-permute-done | bytes 102432 | tf_op jit(solution)/shard_map/ppermute | solution.py:378
  239.6 2.6 collective-permute-start.21
  243.6 1.3 collective-permute-done.21
  244.9 3.2 %collective-permute-start.26 = (bf16[2,40,640]{2,1,0:T(8,128)(2,1)S(1)}, bf16[2,40,640]{2,1,0:T(8,128)(2,1)S(1)}, u32[]{:S(2)}, u32[]{:S(2)}) collective-permute-start(bf16[2,40,640]{2,1,0:T(8,128)(2,1)S(1)} %add_convert_fusion.2), channel_id=1, source_target_pairs={{0,6},{2,4},{4,2},{6,0},{1,7},{3,5},{5,3},{7,1},{8,14},{10,12},{12... | collective-permute-start | bytes 307208 | tf_op jit(solution)/shard_map/ppermute | solution.py:378
  249.3 1.6 pad_maximum_fusion.3
  251.6 4.2 %collective-permute-done.25 = bf16[2,40,640]{2,1,0:T(8,128)(2,1)S(1)} collective-permute-done((bf16[2,40,640]{2,1,0:T(8,128)(2,1)S(1)}, bf16[2,40,640]{2,1,0:T(8,128)(2,1)S(1)}, u32[]{:S(2)}, u32[]{:S(2)}) %collective-permute-start.25) | collective-permute-done | bytes 102432 | tf_op jit(solution)/shard_map/ppermute | solution.py:378
  256.0 1.7 collective-permute-start.29
  257.8 1.3 collective-permute-start.28
  260.0 9.5 %collective-permute-done.29 = bf16[2,160,640]{2,1,0:T(8,128)(2,1)S(1)} collective-permute-done((bf16[2,160,640]{2,1,0:T(8,128)(2,1)S(1)}, bf16[2,160,640]{2,1,0:T(8,128)(2,1)S(1)}, u32[]{:S(2)}, u32[]{:S(2)}) %collective-permute-start.29) | collective-permute-done | bytes 409632 | tf_op jit(solution)/shard_map/ppermute | solution.py:378
  269.4 6.7 %collective-permute-done.28 = bf16[2,160,640]{2,1,0:T(8,128)(2,1)S(1)} collective-permute-done((bf16[2,160,640]{2,1,0:T(8,128)(2,1)S(1)}, bf16[2,160,640]{2,1,0:T(8,128)(2,1)S(1)}, u32[]{:S(2)}, u32[]{:S(2)}) %collective-permute-start.28) | collective-permute-done | bytes 409632 | tf_op jit(solution)/shard_map/ppermute | solution.py:378
  276.6 1.3 pad_maximum_fusion.7
  279.5 4.5 %copy.62 = bf16[1,641,2,720]{3,2,1,0:T(2,128)(2,1)} copy(bf16[1,641,2,720]{1,3,2,0:T(8,128)(2,1)S(1)} %maximum_bitcast_fusion.1) | data formatting | bytes 3692160
  284.0 2.1 broadcast_select_fusion
  286.6 1.7 copy-done.8
  288.3 1.5 multiply_reduce_fusion.1
  291.2 2.5 multiply_reduce_fusion
  296.7 11.8 %fusion.24 = (bf16[641,1282]{1,0:T(8,128)(2,1)}, f32[641,1282]{1,0:T(8,128)}, f32[641,1282]{1,0:T(8,128)}, f32[641,1282]{1,0:T(8,128)}) fusion(f32[641,1282]{1,0:T(8,128)} %param.32, f32[1,1282]{1,0:T(1,128)S(1)} %reshape.204, f32[640,2]{1,0:T(8,128)} %reshape.203, f32[640,1280]{1,0:T(8,128)} %copy-done.8, f32[]{:T(128)S(6)} %min_shard_map.3, ...), kind=kLoop, calls=%fused_computation.126 | loop fusion | flops 15613478 | bytes 24652864 | tf_op jit(solution)/shard_map/convert_element_type | solution.py:632
  309.4 6.8 %convert_bitcast_fusion = (bf16[1282,641]{0,1:T(8,128)(2,1)}, f32[641,1282]{1,0:T(8,128)}, f32[1282,641]{0,1:T(8,128)}, f32[1282,641]{0,1:T(8,128)}) fusion(f32[1282,641]{0,1:T(8,128)S(1)} %copy-done.14, f32[1,1282]{1,0:T(1,128)S(1)} %copy-done.23, f32[640,2]{1,0:T(8,128)S(1)} %copy-done.16, f32[640,1280]{1,0:T(8,128)S(1)} %get-tuple-element.141, ...), kind=kLoop, calls=%fused_computation.29 | loop fusion | flops 15613478 | bytes 24652864 | tf_op jit(solution)/shard_map/transpose | solution.py:633
  (185 shorter events, 34.8 us)
Async XLA Ops:
  13.6 5.3 %copy-start.40 = (s32[8]{0:T(128)S(1)}, s32[8]{0:T(128)}, u32[]{:S(2)}) copy-start(s32[8]{0:T(128)} %param.30) | copy-start | bytes 100
  14.2 19.2 %collective-permute-start.2 = (bf16[2,208,768]{2,1,0:T(8,128)(2,1)S(1)}, bf16[2,208,768]{2,1,0:T(8,128)(2,1)S(1)}, u32[]{:S(2)}, u32[]{:S(2)}) collective-permute-start(bf16[2,208,768]{2,1,0:T(8,128)(2,1)S(1)} %get-tuple-element.156), channel_id=1, source_target_pairs={{0,24},{8,16},{16,8},{24,0},{1,25},{9,17},{17,9},{25,1},{2,26},{10... | collective-permute-start | bytes 1916936 | tf_op jit(solution)/shard_map/ppermute | solution.py:378
  18.2 28.2 %collective-permute-start.1 = (bf16[2,208,768]{2,1,0:T(8,128)(2,1)S(1)}, bf16[2,208,768]{2,1,0:T(8,128)(2,1)}, u32[]{:S(2)}, u32[]{:S(2)}) collective-permute-start(bf16[2,208,768]{2,1,0:T(8,128)(2,1)S(1)} %get-tuple-element.157), channel_id=1, source_target_pairs={{0,16},{8,24},{16,0},{24,8},{1,17},{9,25},{17,1},{25,9},{2,18},{10... | collective-permute-start | bytes 1916936 | tf_op jit(solution)/shard_map/ppermute | solution.py:378
  18.7 28.0 %collective-permute-start = (bf16[2,208,768]{2,1,0:T(8,128)(2,1)S(1)}, bf16[2,208,768]{2,1,0:T(8,128)(2,1)}, u32[]{:S(2)}, u32[]{:S(2)}) collective-permute-start(bf16[2,208,768]{2,1,0:T(8,128)(2,1)S(1)} %get-tuple-element.158), channel_id=1, source_target_pairs={{0,8},{8,0},{16,24},{24,16},{1,9},{9,1},{17,25},{25,17},{2,10},{10... | collective-permute-start | bytes 1916936 | tf_op jit(solution)/shard_map/ppermute | solution.py:378
  48.2 2.0 copy-start
  48.3 6.1 %copy-start.18 = (bf16[641,2,720]{2,1,0:T(2,128)(2,1)S(1)}, bf16[641,2,720]{2,1,0:T(2,128)(2,1)}, u32[]{:S(2)}) copy-start(bf16[641,2,720]{2,1,0:T(2,128)(2,1)} %param.29) | copy-start | bytes 5538244
  50.2 5.7 %copy-start.39 = (s32[9,2]{0,1:T(2,128)S(1)}, s32[9,2]{0,1:T(2,128)}, u32[]{:S(2)}) copy-start(s32[9,2]{0,1:T(2,128)} %param.31) | copy-start | bytes 220
  50.2 17.9 %collective-permute-start.3 = (bf16[4,208,768]{2,1,0:T(8,128)(2,1)}, bf16[4,208,768]{2,1,0:T(8,128)(2,1)}, u32[]{:S(2)}, u32[]{:S(2)}) collective-permute-start(bf16[4,208,768]{2,1,0:T(8,128)(2,1)} %get-tuple-element.154), channel_id=1, source_target_pairs={{0,1},{1,2},{2,3},{3,4},{4,5},{5,6},{6,7},{8,9},{9,10},{10,11},{11... | collective-permute-start | bytes 3833864 | tf_op jit(solution)/shard_map/ppermute | solution.py:459
  53.0 15.0 %collective-permute-start.4 = (bf16[4,208,768]{2,1,0:T(8,128)(2,1)S(1)}, bf16[4,208,768]{2,1,0:T(8,128)(2,1)}, u32[]{:S(2)}, u32[]{:S(2)}) collective-permute-start(bf16[4,208,768]{2,1,0:T(8,128)(2,1)S(1)} %get-tuple-element.153), channel_id=1, source_target_pairs={{1,0},{2,1},{3,2},{4,3},{5,4},{6,5},{7,6},{9,8},{10,9},{11,10},{12... | collective-permute-start | bytes 3833864 | tf_op jit(solution)/shard_map/ppermute | solution.py:460
  60.5 2.8 copy-start.11
  63.5 2.1 copy-start.30
  63.5 3.3 %copy-start.22 = (f32[8,641]{1,0:T(8,128)S(1)}, f32[8,641]{1,0:T(8,128)}, u32[]{:S(2)}) copy-start(f32[8,641]{1,0:T(8,128)} %param.37) | copy-start | bytes 61540
  63.5 3.8 %copy-start.20 = (f32[9,641]{1,0:T(8,128)S(1)}, f32[9,641]{1,0:T(8,128)}, u32[]{:S(2)}) copy-start(f32[9,641]{1,0:T(8,128)} %param.36) | copy-start | bytes 69232
  129.0 19.2 %collective-permute-start.5 = (bf16[4,208,768]{2,1,0:T(8,128)(2,1)}, bf16[4,208,768]{2,1,0:T(8,128)(2,1)S(1)}, u32[]{:S(2)}, u32[]{:S(2)}) collective-permute-start(bf16[4,208,768]{2,1,0:T(8,128)(2,1)} %get-tuple-element.63), channel_id=1, source_target_pairs={{0,1},{1,2},{2,3},{3,4},{4,5},{5,6},{6,7},{8,9},{9,10},{10,11},{11... | collective-permute-start | bytes 3833864 | tf_op jit(solution)/shard_map/ppermute | solution.py:495
  135.7 13.5 %collective-permute-start.6 = (bf16[4,208,768]{2,1,0:T(8,128)(2,1)}, bf16[4,208,768]{2,1,0:T(8,128)(2,1)S(1)}, u32[]{:S(2)}, u32[]{:S(2)}) collective-permute-start(bf16[4,208,768]{2,1,0:T(8,128)(2,1)} %get-tuple-element.64), channel_id=1, source_target_pairs={{1,0},{2,1},{3,2},{4,3},{5,4},{6,5},{7,6},{9,8},{10,9},{11,10},{12... | collective-permute-start | bytes 3833864 | tf_op jit(solution)/shard_map/ppermute | solution.py:496
  144.1 6.1 %copy-start.1 = (bf16[4,2,208,768]{3,2,1,0:T(8,128)(2,1)S(1)}, bf16[4,2,208,768]{3,2,1,0:T(8,128)(2,1)}, u32[]{:S(2)}) copy-start(bf16[4,2,208,768]{3,2,1,0:T(8,128)(2,1)} %copy-done) | copy-start | bytes 7667716
  144.2 6.1 %copy-start.2 = (bf16[1536,768]{1,0:T(8,128)(2,1)S(1)}, bf16[1536,768]{1,0:T(8,128)(2,1)}, u32[]{:S(2)}) copy-start(bf16[1536,768]{1,0:T(8,128)(2,1)} %get-tuple-element.65.bg_ref) | copy-start | bytes 7077892
  144.2 6.1 %copy-start.7 = (f32[1,768]{1,0:T(1,128)S(1)}, f32[1,768]{1,0:T(1,128)}, u32[]{:S(2)}) copy-start(f32[1,768]{1,0:T(1,128)} %pad.53.gain_ref) | copy-start | bytes 9220
  161.2 8.0 %collective-permute-start.7 = (f32[152,128]{1,0:T(8,128)S(1)}, f32[152,128]{1,0:T(8,128)S(1)}, u32[]{:S(2)}, u32[]{:S(2)}) collective-permute-start(f32[152,128]{1,0:T(8,128)S(1)} %pad_bitcast_fusion), channel_id=1, source_target_pairs={{0,1},{1,0},{2,3},{3,2},{4,5},{5,4},{6,7},{7,6},{8,9},{9,8},{10,11... | collective-permute-start | bytes 233480 | tf_op jit(solution)/shard_map/ppermute | solution.py:551
  169.2 19.2 %collective-permute-start.17 = (bf16[2,640,640]{2,1,0:T(8,128)(2,1)}, bf16[2,640,640]{2,1,0:T(8,128)(2,1)}, u32[]{:S(2)}, u32[]{:S(2)}) collective-permute-start(bf16[2,640,640]{2,1,0:T(8,128)(2,1)} %fusion.7), channel_id=1, source_target_pairs={{0,1},{1,0},{2,3},{3,2},{4,5},{5,4},{6,7},{7,6},{8,9},{9,8},{10,11... | collective-permute-start | bytes 4915208 | tf_op jit(solution)/shard_map/ppermute | solution.py:524
  169.2 5.8 %collective-permute-start.10 = (f32[152,128]{1,0:T(8,128)S(1)}, f32[152,128]{1,0:T(8,128)S(1)}, u32[]{:S(2)}, u32[]{:S(2)}) collective-permute-start(f32[152,128]{1,0:T(8,128)S(1)} %fusion.20), channel_id=1, source_target_pairs={{0,24},{8,16},{16,8},{24,0},{1,25},{9,17},{17,9},{25,1},{2,26},{10... | collective-permute-start | bytes 233480 | tf_op jit(solution)/shard_map/ppermute | solution.py:378
  171.0 5.6 %collective-permute-start.9 = (f32[152,128]{1,0:T(8,128)S(1)}, f32[152,128]{1,0:T(8,128)S(1)}, u32[]{:S(2)}, u32[]{:S(2)}) collective-permute-start(f32[152,128]{1,0:T(8,128)S(1)} %fusion.20), channel_id=1, source_target_pairs={{0,16},{8,24},{16,0},{24,8},{1,17},{9,25},{17,1},{25,9},{2,18},{10... | collective-permute-start | bytes 233480 | tf_op jit(solution)/shard_map/ppermute | solution.py:378
  172.2 4.4 %collective-permute-start.8 = (f32[152,128]{1,0:T(8,128)S(1)}, f32[152,128]{1,0:T(8,128)S(1)}, u32[]{:S(2)}, u32[]{:S(2)}) collective-permute-start(f32[152,128]{1,0:T(8,128)S(1)} %fusion.20), channel_id=1, source_target_pairs={{0,8},{8,0},{16,24},{24,16},{1,9},{9,1},{17,25},{25,17},{2,10},{10... | collective-permute-start | bytes 233480 | tf_op jit(solution)/shard_map/ppermute | solution.py:378
  176.7 7.4 %collective-permute-start.13 = (f32[152,128]{1,0:T(8,128)S(1)}, f32[152,128]{1,0:T(8,128)S(1)}, u32[]{:S(2)}, u32[]{:S(2)}) collective-permute-start(f32[152,128]{1,0:T(8,128)S(1)} %add_add_fusion), channel_id=1, source_target_pairs={{0,6},{2,4},{4,2},{6,0},{1,7},{3,5},{5,3},{7,1},{8,14},{10,12},{12... | collective-permute-start | bytes 233480 | tf_op jit(solution)/shard_map/ppermute | solution.py:378
  179.2 7.9 %collective-permute-start.12 = (f32[152,128]{1,0:T(8,128)S(1)}, f32[152,128]{1,0:T(8,128)S(1)}, u32[]{:S(2)}, u32[]{:S(2)}) collective-permute-start(f32[152,128]{1,0:T(8,128)S(1)} %add_add_fusion), channel_id=1, source_target_pairs={{0,4},{2,6},{4,0},{6,2},{1,5},{3,7},{5,1},{7,3},{8,12},{10,14},{12... | collective-permute-start | bytes 233480 | tf_op jit(solution)/shard_map/ppermute | solution.py:378
  179.8 7.2 %collective-permute-start.11 = (f32[152,128]{1,0:T(8,128)S(1)}, f32[152,128]{1,0:T(8,128)S(1)}, u32[]{:S(2)}, u32[]{:S(2)}) collective-permute-start(f32[152,128]{1,0:T(8,128)S(1)} %add_add_fusion), channel_id=1, source_target_pairs={{0,2},{2,0},{4,6},{6,4},{1,3},{3,1},{5,7},{7,5},{8,10},{10,8},{12,... | collective-permute-start | bytes 233480 | tf_op jit(solution)/shard_map/ppermute | solution.py:378
  181.1 7.2 %copy-start.9 = (bf16[1,640,1280]{2,1,0:T(8,128)(2,1)S(1)}, bf16[1,640,1280]{2,1,0:T(8,128)(2,1)}, u32[]{:S(2)}) copy-start(bf16[1,640,1280]{2,1,0:T(8,128)(2,1)} %get-tuple-element.196) | copy-start | bytes 4915204
  181.1 7.2 %copy-start.10 = (bf16[1,640,1280]{2,1,0:T(8,128)(2,1)S(1)}, bf16[1,640,1280]{2,1,0:T(8,128)(2,1)}, u32[]{:S(2)}) copy-start(bf16[1,640,1280]{2,1,0:T(8,128)(2,1)} %get-tuple-element.197) | copy-start | bytes 4915204
  182.4 66.3 %collective-permute-start.16 = (bf16[2,208,768]{2,1,0:T(8,128)(2,1)}, bf16[2,208,768]{2,1,0:T(8,128)(2,1)}, u32[]{:S(2)}, u32[]{:S(2)}) collective-permute-start(bf16[2,208,768]{2,1,0:T(8,128)(2,1)} %get-tuple-element.150), channel_id=1, source_target_pairs={{0,24},{8,16},{16,8},{24,0},{1,25},{9,17},{17,9},{25,1},{2,26},{10... | collective-permute-start | bytes 1916936 | tf_op jit(solution)/shard_map/ppermute | solution.py:378
  184.1 65.3 %collective-permute-start.15 = (bf16[2,208,768]{2,1,0:T(8,128)(2,1)}, bf16[2,208,768]{2,1,0:T(8,128)(2,1)}, u32[]{:S(2)}, u32[]{:S(2)}) collective-permute-start(bf16[2,208,768]{2,1,0:T(8,128)(2,1)} %get-tuple-element.151), channel_id=1, source_target_pairs={{0,16},{8,24},{16,0},{24,8},{1,17},{9,25},{17,1},{25,9},{2,18},{10... | collective-permute-start | bytes 1916936 | tf_op jit(solution)/shard_map/ppermute | solution.py:378
  191.2 18.6 %collective-permute-start.20 = (bf16[2,160,640]{2,1,0:T(8,128)(2,1)}, bf16[2,160,640]{2,1,0:T(8,128)(2,1)}, u32[]{:S(2)}, u32[]{:S(2)}) collective-permute-start(bf16[2,160,640]{2,1,0:T(8,128)(2,1)} %get-tuple-element.164), channel_id=1, source_target_pairs={{0,24},{8,16},{16,8},{24,0},{1,25},{9,17},{17,9},{25,1},{2,26},{10... | collective-permute-start | bytes 1228808 | tf_op jit(solution)/shard_map/ppermute | solution.py:378
  192.8 37.5 %collective-permute-start.19 = (bf16[2,160,640]{2,1,0:T(8,128)(2,1)S(1)}, bf16[2,160,640]{2,1,0:T(8,128)(2,1)}, u32[]{:S(2)}, u32[]{:S(2)}) collective-permute-start(bf16[2,160,640]{2,1,0:T(8,128)(2,1)S(1)} %get-tuple-element.165), channel_id=1, source_target_pairs={{0,16},{8,24},{16,0},{24,8},{1,17},{9,25},{17,1},{25,9},{2,18},{10... | collective-permute-start | bytes 1228808 | tf_op jit(solution)/shard_map/ppermute | solution.py:378
  194.1 36.2 %collective-permute-start.18 = (bf16[2,160,640]{2,1,0:T(8,128)(2,1)S(1)}, bf16[2,160,640]{2,1,0:T(8,128)(2,1)}, u32[]{:S(2)}, u32[]{:S(2)}) collective-permute-start(bf16[2,160,640]{2,1,0:T(8,128)(2,1)S(1)} %get-tuple-element.163), channel_id=1, source_target_pairs={{0,8},{8,0},{16,24},{24,16},{1,9},{9,1},{17,25},{25,17},{2,10},{10... | collective-permute-start | bytes 1228808 | tf_op jit(solution)/shard_map/ppermute | solution.py:378
  197.4 53.5 %copy-start.28 = (f32[1,641]{1,0:T(1,128)}, f32[1,641]{1,0:T(1,128)S(1)}, u32[]{:S(2)}) copy-start(f32[1,641]{1,0:T(1,128)S(1)} %stack.97) | copy-start | bytes 7696
  209.8 39.6 %collective-permute-start.14 = (bf16[2,208,768]{2,1,0:T(8,128)(2,1)}, bf16[2,208,768]{2,1,0:T(8,128)(2,1)S(1)}, u32[]{:S(2)}, u32[]{:S(2)}) collective-permute-start(bf16[2,208,768]{2,1,0:T(8,128)(2,1)} %get-tuple-element.152), channel_id=1, source_target_pairs={{0,8},{8,0},{16,24},{24,16},{1,9},{9,1},{17,25},{25,17},{2,10},{10... | collective-permute-start | bytes 1916936 | tf_op jit(solution)/shard_map/ppermute | solution.py:378
  231.9 7.7 %collective-permute-start.23 = (bf16[2,40,640]{2,1,0:T(8,128)(2,1)S(1)}, bf16[2,40,640]{2,1,0:T(8,128)(2,1)S(1)}, u32[]{:S(2)}, u32[]{:S(2)}) collective-permute-start(bf16[2,40,640]{2,1,0:T(8,128)(2,1)S(1)} %get-tuple-element.181), channel_id=1, source_target_pairs={{0,6},{2,4},{4,2},{6,0},{1,7},{3,5},{5,3},{7,1},{8,14},{10,12},{12... | collective-permute-start | bytes 307208 | tf_op jit(solution)/shard_map/ppermute | solution.py:378
  234.4 9.2 %collective-permute-start.22 = (bf16[2,40,640]{2,1,0:T(8,128)(2,1)S(1)}, bf16[2,40,640]{2,1,0:T(8,128)(2,1)S(1)}, u32[]{:S(2)}, u32[]{:S(2)}) collective-permute-start(bf16[2,40,640]{2,1,0:T(8,128)(2,1)S(1)} %get-tuple-element.182), channel_id=1, source_target_pairs={{0,4},{2,6},{4,0},{6,2},{1,5},{3,7},{5,1},{7,3},{8,12},{10,14},{12... | collective-permute-start | bytes 307208 | tf_op jit(solution)/shard_map/ppermute | solution.py:378
  239.6 5.3 %collective-permute-start.21 = (bf16[2,40,640]{2,1,0:T(8,128)(2,1)S(1)}, bf16[2,40,640]{2,1,0:T(8,128)(2,1)S(1)}, u32[]{:S(2)}, u32[]{:S(2)}) collective-permute-start(bf16[2,40,640]{2,1,0:T(8,128)(2,1)S(1)} %get-tuple-element.180), channel_id=1, source_target_pairs={{0,2},{2,0},{4,6},{6,4},{1,3},{3,1},{5,7},{7,5},{8,10},{10,8},{12,... | collective-permute-start | bytes 307208 | tf_op jit(solution)/shard_map/ppermute | solution.py:378
  244.9 6.7 %collective-permute-start.26 = (bf16[2,40,640]{2,1,0:T(8,128)(2,1)S(1)}, bf16[2,40,640]{2,1,0:T(8,128)(2,1)S(1)}, u32[]{:S(2)}, u32[]{:S(2)}) collective-permute-start(bf16[2,40,640]{2,1,0:T(8,128)(2,1)S(1)} %add_convert_fusion.2), channel_id=1, source_target_pairs={{0,6},{2,4},{4,2},{6,0},{1,7},{3,5},{5,3},{7,1},{8,14},{10,12},{12... | collective-permute-start | bytes 307208 | tf_op jit(solution)/shard_map/ppermute | solution.py:378
  248.1 7.7 %collective-permute-start.25 = (bf16[2,40,640]{2,1,0:T(8,128)(2,1)S(1)}, bf16[2,40,640]{2,1,0:T(8,128)(2,1)S(1)}, u32[]{:S(2)}, u32[]{:S(2)}) collective-permute-start(bf16[2,40,640]{2,1,0:T(8,128)(2,1)S(1)} %add_convert_fusion.2), channel_id=1, source_target_pairs={{0,4},{2,6},{4,0},{6,2},{1,5},{3,7},{5,1},{7,3},{8,12},{10,14},{12... | collective-permute-start | bytes 307208 | tf_op jit(solution)/shard_map/ppermute | solution.py:378
  248.7 7.1 %collective-permute-start.24 = (bf16[2,40,640]{2,1,0:T(8,128)(2,1)S(1)}, bf16[2,40,640]{2,1,0:T(8,128)(2,1)S(1)}, u32[]{:S(2)}, u32[]{:S(2)}) collective-permute-start(bf16[2,40,640]{2,1,0:T(8,128)(2,1)S(1)} %add_convert_fusion.2), channel_id=1, source_target_pairs={{0,2},{2,0},{4,6},{6,4},{1,3},{3,1},{5,7},{7,5},{8,10},{10,8},{12,... | collective-permute-start | bytes 307208 | tf_op jit(solution)/shard_map/ppermute | solution.py:378
  256.0 13.4 %collective-permute-start.29 = (bf16[2,160,640]{2,1,0:T(8,128)(2,1)S(1)}, bf16[2,160,640]{2,1,0:T(8,128)(2,1)S(1)}, u32[]{:S(2)}, u32[]{:S(2)}) collective-permute-start(bf16[2,160,640]{2,1,0:T(8,128)(2,1)S(1)} %get-tuple-element.175), channel_id=1, source_target_pairs={{0,24},{8,16},{16,8},{24,0},{1,25},{9,17},{17,9},{25,1},{2,26},{10... | collective-permute-start | bytes 1228808 | tf_op jit(solution)/shard_map/ppermute | solution.py:378
  257.8 18.4 %collective-permute-start.28 = (bf16[2,160,640]{2,1,0:T(8,128)(2,1)S(1)}, bf16[2,160,640]{2,1,0:T(8,128)(2,1)S(1)}, u32[]{:S(2)}, u32[]{:S(2)}) collective-permute-start(bf16[2,160,640]{2,1,0:T(8,128)(2,1)S(1)} %get-tuple-element.175), channel_id=1, source_target_pairs={{0,16},{8,24},{16,0},{24,8},{1,17},{9,25},{17,1},{25,9},{2,18},{10... | collective-permute-start | bytes 1228808 | tf_op jit(solution)/shard_map/ppermute | solution.py:378
  259.0 17.1 %collective-permute-start.27 = (bf16[2,160,640]{2,1,0:T(8,128)(2,1)S(1)}, bf16[2,160,640]{2,1,0:T(8,128)(2,1)S(1)}, u32[]{:S(2)}, u32[]{:S(2)}) collective-permute-start(bf16[2,160,640]{2,1,0:T(8,128)(2,1)S(1)} %get-tuple-element.175), channel_id=1, source_target_pairs={{0,8},{8,0},{16,24},{24,16},{1,9},{9,1},{17,25},{25,17},{2,10},{10... | collective-permute-start | bytes 1228808 | tf_op jit(solution)/shard_map/ppermute | solution.py:378
  277.9 6.1 %collective-permute-start.30 = (bf16[2,640,640]{2,1,0:T(8,128)(2,1)}, bf16[2,640,640]{2,1,0:T(8,128)(2,1)}, u32[]{:S(2)}, u32[]{:S(2)}) collective-permute-start(bf16[2,640,640]{2,1,0:T(8,128)(2,1)} %pad_maximum_fusion.7), channel_id=1, source_target_pairs={{0,1},{1,0},{2,3},{3,2},{4,5},{5,4},{6,7},{7,6},{8,9},{9,8},{10,11... | collective-permute-start | bytes 4915208 | tf_op jit(solution)/shard_map/ppermute | solution.py:530
  286.1 2.2 copy-start.17
  286.6 1.7 copy-start.8
  286.6 4.5 %copy-start.23 = (f32[1,1282]{1,0:T(1,128)S(1)}, f32[1,1282]{1,0:T(1,128)}, u32[]{:S(2)}) copy-start(f32[1,1282]{1,0:T(1,128)} %reshape.206) | copy-start | bytes 15388
  296.6 11.9 %copy-start.27 = (f32[1282]{0:T(1024)S(1)}, f32[1282]{0:T(1024)}, u32[]{:S(2)}) copy-start(f32[1282]{0:T(1024)} %param.33) | copy-start | bytes 15388
  296.6 11.9 %copy-start.34 = (f32[1282]{0:T(1024)S(1)}, f32[1282]{0:T(1024)}, u32[]{:S(2)}) copy-start(f32[1282]{0:T(1024)} %param.40) | copy-start | bytes 15388
  296.6 11.9 %copy-start.35 = (f32[1282]{0:T(1024)S(1)}, f32[1282]{0:T(1024)}, u32[]{:S(2)}) copy-start(f32[1282]{0:T(1024)} %param.41) | copy-start | bytes 15388
  296.7 12.6 %copy-start.12 = (f32[1282,641]{0,1:T(8,128)S(1)}, f32[1282,641]{0,1:T(8,128)}, u32[]{:S(2)}) copy-start(f32[1282,641]{0,1:T(8,128)} %param.34) | copy-start | bytes 9861148
  296.7 12.6 %copy-start.14 = (f32[1282,641]{0,1:T(8,128)S(1)}, f32[1282,641]{0,1:T(8,128)}, u32[]{:S(2)}) copy-start(f32[1282,641]{0,1:T(8,128)} %param.43) | copy-start | bytes 9861148
  296.7 12.6 %copy-start.15 = (f32[1282,641]{0,1:T(8,128)S(1)}, f32[1282,641]{0,1:T(8,128)}, u32[]{:S(2)}) copy-start(f32[1282,641]{0,1:T(8,128)} %param.42) | copy-start | bytes 9861148
  296.7 12.6 %copy-start.16 = (f32[640,2]{1,0:T(8,128)S(1)}, f32[640,2]{1,0:T(8,128)}, u32[]{:S(2)}) copy-start(f32[640,2]{1,0:T(8,128)} %reshape.205) | copy-start | bytes 15364
  309.3 6.9 %copy-start.29 = (f32[1,641]{1,0:T(1,128)S(1)}, f32[1,641]{1,0:T(1,128)}, u32[]{:S(2)}) copy-start(f32[1,641]{1,0:T(1,128)} %copy-done.28) | copy-start | bytes 7696
  309.3 6.9 %copy-start.31 = (f32[2,641]{1,0:T(2,128)S(1)}, f32[2,641]{1,0:T(2,128)}, u32[]{:S(2)}) copy-start(f32[2,641]{1,0:T(2,128)} %param.35) | copy-start | bytes 15388
  309.3 6.9 %copy-start.36 = (f32[2,641]{1,0:T(2,128)S(1)}, f32[2,641]{1,0:T(2,128)}, u32[]{:S(2)}) copy-start(f32[2,641]{1,0:T(2,128)} %param.44) | copy-start | bytes 15388
  309.3 6.9 %copy-start.37 = (f32[2,641]{1,0:T(2,128)S(1)}, f32[2,641]{1,0:T(2,128)}, u32[]{:S(2)}) copy-start(f32[2,641]{1,0:T(2,128)} %param.45) | copy-start | bytes 15388
  309.3 7.6 %copy-start.21 = (f32[9,641]{1,0:T(8,128)S(1)}, f32[9,641]{1,0:T(8,128)}, u32[]{:S(2)}) copy-start(f32[9,641]{1,0:T(8,128)} %param.36) | copy-start | bytes 69232
  309.4 7.5 %copy-start.24 = (f32[9,641]{1,0:T(8,128)S(1)}, f32[9,641]{1,0:T(8,128)}, u32[]{:S(2)}) copy-start(f32[9,641]{1,0:T(8,128)} %param.46) | copy-start | bytes 69232
  309.4 7.5 %copy-start.25 = (f32[9,641]{1,0:T(8,128)S(1)}, f32[9,641]{1,0:T(8,128)}, u32[]{:S(2)}) copy-start(f32[9,641]{1,0:T(8,128)} %param.47) | copy-start | bytes 69232
  309.4 8.2 %copy-start.32 = (f32[8,641]{1,0:T(8,128)S(1)}, f32[8,641]{1,0:T(8,128)}, u32[]{:S(2)}) copy-start(f32[8,641]{1,0:T(8,128)} %param.48) | copy-start | bytes 61540
  309.4 8.2 %copy-start.33 = (f32[8,641]{1,0:T(8,128)S(1)}, f32[8,641]{1,0:T(8,128)}, u32[]{:S(2)}) copy-start(f32[8,641]{1,0:T(8,128)} %param.49) | copy-start | bytes 61540
  (8 other events, 9.0 us)
